TPU v7x, 256 devices: a whole 4x4x8 slice. The times are simulated.
256 devices in a mesh: tile: 32 (over x, y, core), cuts: 8 (over z).
Axes of the slice: x: 4, y: 4, z: 8, core: 2. Of those that a mesh axis runs over, the one named last changes fastest.
Arguments:
- object_real: float32 [16, 4096, 2048], P('cuts', 'tile'), may hold values from 0.8 to 1.1
- object_imag: float32 [16, 4096, 2048], P('cuts', 'tile'), may hold values from -1.5 to 1.5
- probe: float32 [2, 128, 128], replicated, may hold values from -6 to 6
- positions: int32 [128, 2], P('tile'), may hold values from 0 to 4095, as said below
- counts: int32 [128, 128, 128], P('tile'), may hold values from 0 to 3
Outputs:
- grad_real: float32 [16, 4096, 2048], P('cuts', 'tile')
- grad_imag: float32 [16, 4096, 2048], P('cuts', 'tile')
Inputs may be any that keep to these rules, and one draw needn't show every extreme that they name: `positions`: position k has its row within 128 * (k // 4) to 128 * (k // 4) + 127 and its column within 0 to 1920.
All inputs are finite; a program needn't handle non-finite values.
Results may differ from a plain program's by a relative error of at most 0.0003.
Values sent between devices are 32-bit elements; how exact they have to be, the bound alone decides.
A program may use at most 128 MiB of HBM per device.

v0:
```python
import math

import jax
import jax.numpy as jnp
from jax import lax
from jax.sharding import PartitionSpec as P

phase_scale = 32.0


def shifted(value, axis, steps):
    count = lax.axis_size(axis)
    pairs = [(source, (source + steps) % count) for source in range(count)]
    return lax.ppermute(value, axis, pairs)


def from_behind(shard, axis, by):
    peers = lax.axis_size(axis)
    pairs = [(i, i + by) for i in range(peers) if 0 <= i + by < peers]
    return lax.ppermute(shard, axis, pairs)


def dft_tables(window):
    index_int = jnp.arange(window, dtype=jnp.int32)
    product = index_int[:, None] * index_int[None, :] % window
    angle = 2.0 * math.pi / window * product.astype(jnp.float32)
    norm_factor = 1.0 / math.sqrt(window)
    cos_table = jnp.cos(angle) * norm_factor
    sin_table = -jnp.sin(angle) * norm_factor
    freq = jnp.where(index_int < window // 2, index_int, index_int - window).astype(jnp.float32)
    chirp = phase_scale * (freq[:, None] ** 2 + freq[None, :] ** 2) / (window * window)
    return (cos_table, sin_table, jnp.cos(chirp), -jnp.sin(chirp))


def left_times(matrix, field):
    return jnp.einsum("jk,...kl->...jl", matrix, field, precision=lax.Precision.HIGHEST)


def right_times(field, matrix):
    return jnp.einsum("...jk,kl->...jl", field, matrix, precision=lax.Precision.HIGHEST)


def transform(real_part, imag_part, cos_table, sin_table, sign):
    sin_signed = sign * sin_table
    left_re = left_times(cos_table, real_part) - left_times(sin_signed, imag_part)
    left_im = left_times(cos_table, imag_part) + left_times(sin_signed, real_part)
    out_re = right_times(left_re, cos_table) - right_times(left_im, sin_signed)
    out_im = right_times(left_re, sin_signed) + right_times(left_im, cos_table)
    return (out_re, out_im)


def propagate(real_part, imag_part, tables, sign):
    cos_table, sin_table, phase_re, phase_im = tables
    freq_re, freq_im = transform(real_part, imag_part, cos_table, sin_table, 1.0)
    turned_re = phase_re * freq_re - sign * phase_im * freq_im
    turned_im = phase_re * freq_im + sign * phase_im * freq_re
    return transform(turned_re, turned_im, cos_table, sin_table, -1.0)


def shards(object_real, object_imag, probe, positions, counts):
    cut_count = lax.axis_size("cuts")
    section_index = lax.axis_index("cuts")
    tile_index = lax.axis_index("tile")
    slice_count, strip_rows, col_count = object_real.shape
    window = probe.shape[1]
    pos_count = positions.shape[0]
    tables = dft_tables(window)
    cos_table, sin_table = (tables[0], tables[1])
    strip = jnp.stack([object_real, object_imag], 1)
    row_starts = positions[:, 0] - tile_index * strip_rows
    col_starts = positions[:, 1]
    batch_size = 1
    group_count = pos_count // batch_size
    step_count = cut_count + group_count - 1
    rim_part = shifted(strip, "tile", -1)
    extended = jnp.concatenate([strip, rim_part], 2)

    def windows(slot_start):
        row_pick = lax.dynamic_slice_in_dim(row_starts, slot_start, batch_size, 0)
        col_pick = lax.dynamic_slice_in_dim(col_starts, slot_start, batch_size, 0)
        return jax.vmap(
            lambda row_at, col_at: lax.dynamic_slice(
                extended, (0, 0, row_at, col_at), (slice_count, 2, window, window)
            )
        )(row_pick, col_pick)

    def forward_step(state_tuple, tick_index):
        current, saved, exit_waves = state_tuple
        group_index = tick_index - section_index
        active = (group_index >= 0) & (group_index < group_count)
        slot_start = jnp.clip(group_index, 0, group_count - 1) * batch_size
        start_wave = probe[None]
        wave = jnp.where(section_index == 0, start_wave, current)
        patches = windows(slot_start)
        wave_re, wave_im = (wave[:, 0], wave[:, 1])
        kept = []
        for layer in range(slice_count):
            kept.append(jnp.stack([wave_re, wave_im], 1))
            patch_re, patch_im = (patches[:, layer, 0], patches[:, layer, 1])
            mixed_re = patch_re * wave_re - patch_im * wave_im
            mixed_im = patch_re * wave_im + patch_im * wave_re
            wave_re, wave_im = propagate(mixed_re, mixed_im, tables, 1.0)
        leaving = jnp.stack([wave_re, wave_im], 1)
        record = jnp.stack(kept, 1)
        saved = jnp.where(
            active, lax.dynamic_update_slice(saved, record, (slot_start, 0, 0, 0, 0)), saved
        )
        exit_waves = jnp.where(
            active & (section_index == cut_count - 1),
            lax.dynamic_update_slice(exit_waves, leaving, (slot_start, 0, 0, 0)),
            exit_waves,
        )
        current = from_behind(leaving, "cuts", 1)
        return ((current, saved, exit_waves), None)

    start_state = (
        jnp.zeros((batch_size, 2, window, window), jnp.float32),
        jnp.zeros((pos_count, slice_count, 2, window, window), jnp.float32),
        jnp.zeros((pos_count, 2, window, window), jnp.float32),
    )
    (unused_wave, saved, exit_waves), unused = lax.scan(
        forward_step, start_state, jnp.arange(step_count)
    )
    far_re, far_im = transform(exit_waves[:, 0], exit_waves[:, 1], cos_table, sin_table, 1.0)
    weight = 4.0 * (far_re * far_re + far_im * far_im - counts.astype(jnp.float32))
    detect_re, detect_im = transform(weight * far_re, weight * far_im, cos_table, sin_table, -1.0)
    detector = jnp.stack([detect_re, detect_im], 1)
    rim_shape = (1, slice_count, 2, 1, 1)

    def backward_step(state_tuple, tick_index):
        current, grads, rim_sums = state_tuple
        group_index = tick_index - (cut_count - 1 - section_index)
        active = (group_index >= 0) & (group_index < group_count)
        slot_start = jnp.clip(group_index, 0, group_count - 1) * batch_size
        entering = jnp.where(
            section_index == cut_count - 1,
            lax.dynamic_slice_in_dim(detector, slot_start, batch_size, 0),
            current,
        )
        patches = windows(slot_start)
        record = lax.dynamic_slice_in_dim(saved, slot_start, batch_size, 0)
        grad_re, grad_im = (entering[:, 0], entering[:, 1])
        pieces = [None] * slice_count
        for layer in range(slice_count - 1, -1, -1):
            back_re, back_im = propagate(grad_re, grad_im, tables, -1.0)
            kept_re, kept_im = (record[:, layer, 0], record[:, layer, 1])
            pieces[layer] = jnp.stack(
                [kept_re * back_re + kept_im * back_im, kept_re * back_im - kept_im * back_re], 1
            )
            patch_re, patch_im = (patches[:, layer, 0], patches[:, layer, 1])
            grad_re = patch_re * back_re + patch_im * back_im
            grad_im = patch_re * back_im - patch_im * back_re
        contrib = jnp.stack(pieces, 1) * active.astype(jnp.float32)

        def add_one(member, total):
            row_at = row_starts[slot_start + member]
            col_at = col_starts[slot_start + member]
            region = lax.dynamic_slice(
                total, (0, 0, row_at, col_at), (slice_count, 2, window, window)
            )
            return lax.dynamic_update_slice(total, region + contrib[member], (0, 0, row_at, col_at))

        grads = lax.fori_loop(0, batch_size, add_one, grads)
        current = from_behind(jnp.stack([grad_re, grad_im], 1), "cuts", -1)
        return ((current, grads, rim_sums), None)

    back_state = (
        jnp.zeros((batch_size, 2, window, window), jnp.float32),
        jnp.zeros((slice_count, 2, strip_rows + window, col_count), jnp.float32),
        jnp.zeros(rim_shape, jnp.float32),
    )
    (unused_grad, grads, rim_sums), unused = lax.scan(
        backward_step, back_state, jnp.arange(step_count)
    )
    total = grads[:, :, :strip_rows, :]
    lower_part = shifted(grads[:, :, strip_rows:, :], "tile", 1)
    total = total.at[:, :, :window, :].add(lower_part)
    return (total[:, 0], total[:, 1])


def solution(mesh):
    placed = (
        P("cuts", "tile", None),
        P("cuts", "tile", None),
        P(),
        P("tile", None),
        P("tile", None, None),
    )
    return jax.shard_map(
        shards,
        mesh=mesh,
        in_specs=placed,
        out_specs=(P("cuts", "tile", None), P("cuts", "tile", None)),
        check_vma=False,
    )
```

profile of v0, /device:TPU:224, one launch (start us, length us, event | category | flops | bytes accessed | tf_op | source)
XLA Modules:
  0.0 912.2 jit_solution(9541988867662811751)
XLA Ops:
  0.6 4.8 pad_maximum_fusion.3
  5.5 4.6 collective-permute-start.2
  10.2 46.3 %collective-permute-done.2 = f32[2,2,128,2048]{3,2,1,0:T(8,128)} collective-permute-done((f32[2,2,128,2048]{3,2,1,0:T(8,128)}, f32[2,2,128,2048]{3,2,1,0:T(8,128)}, u32[]{:S(2)}, u32[]{:S(2)}) %collective-permute-start.2) | collective-permute-done | bytes 4194336 | tf_op jit(solution)/shard_map/ppermute | solution.py:14
  56.5 5.5 pad_maximum_fusion.2
  62.2 368.9 %while.44 = (s32[]{:T(128)}, f32[1,2,128,128]{3,2,1,0:T(8,128)S(1)}, f32[4,2,2,128,128]{4,3,2,1,0:T(8,128)S(1)}, f32[4,2,128,128]{2,3,0,1:T(8,128)S(1)}, s32[11]...) while((s32[]{:T(128)}, ...), condition=%wide.region_1.2_spmd.clone.clone.clone, body=%wide.region_0.1_spmd.clone.clone.clone.sunk | while | flops 814940160 | bytes 10555860 | solution.py:121
  88.2 1.3 collective-permute-start
  89.7 5.4 collective-permute-done
  121.0 1.3 collective-permute-start
  122.5 5.4 collective-permute-done
  153.9 1.3 collective-permute-start
  155.4 5.4 collective-permute-done
  186.8 1.3 collective-permute-start
  188.3 5.4 collective-permute-done
  219.6 1.3 collective-permute-start
  221.1 5.4 collective-permute-done
  252.5 1.3 collective-permute-start
  254.0 6.0 collective-permute-done
  286.0 1.3 collective-permute-start
  287.5 6.6 collective-permute-done
  320.0 1.3 collective-permute-start
  321.5 6.9 collective-permute-done
  354.5 1.3 collective-permute-start
  356.0 6.6 collective-permute-done
  388.7 1.3 collective-permute-start
  390.2 6.6 collective-permute-done
  422.8 1.3 collective-permute-start
  424.3 6.6 collective-permute-done
  442.6 4.3 broadcast_in_dim.34.clone
  446.9 407.5 %while.45 = (s32[]{:T(128)}, f32[1,2,128,128]{3,2,1,0:T(8,128)S(1)}, f32[2,2,256,2048]{3,2,0,1:T(8,128)}, s32[11]{0:T(128)S(1)}, s32[]{:T(128)}, /*index=5*/s32[...) while((s32[]{:T(128)}, ...), condition=%wide.region_3.4_spmd.clone.clone.clone, body=%wide.region_2.3_spmd.clone.clone.clone.sunk | while | flops 815398912 | bytes 10555972 | solution.py:172
  472.6 5.1 collective-permute-start.1
  482.5 2.9 dynamic_update_slice.12
  511.0 5.0 collective-permute-start.1
  519.6 1.2 fusion.941
  520.9 4.2 dynamic_update_slice.12
  550.7 3.7 collective-permute-start.1
  558.0 1.2 fusion.941
  559.3 4.0 dynamic_update_slice.12
  588.8 2.2 collective-permute-start.1
  594.6 1.2 fusion.941
  595.9 4.0 dynamic_update_slice.12
  625.4 1.9 collective-permute-start.1
  630.9 1.2 fusion.941
  632.2 4.0 dynamic_update_slice.12
  661.8 1.9 collective-permute-start.1
  667.3 1.2 fusion.941
  668.6 4.0 dynamic_update_slice.12
  698.1 1.9 collective-permute-start.1
  703.7 1.2 fusion.941
  704.9 4.0 dynamic_update_slice.12
  734.5 1.9 collective-permute-start.1
  740.1 1.2 fusion.941
  741.3 4.0 dynamic_update_slice.12
  770.9 1.9 collective-permute-start.1
  776.5 1.2 fusion.941
  777.7 4.0 dynamic_update_slice.12
  807.3 1.9 collective-permute-start.1
  812.8 1.2 fusion.941
  814.1 4.0 dynamic_update_slice.12
  843.6 1.9 collective-permute-start.1
  849.2 1.2 fusion.941
  850.5 4.0 dynamic_update_slice.12
  854.5 2.6 slice.128
  857.2 51.2 %collective-permute-done.3 = f32[2,2,128,2048]{3,2,0,1:T(8,128)S(1)} collective-permute-done((f32[2,2,128,2048]{3,2,0,1:T(8,128)S(1)}, f32[2,2,128,2048]{3,2,0,1:T(8,128)S(1)}, u32[]{:S(2)}, u32[]{:S(2)}) %collective-permute-start.3) | collective-permute-done | bytes 4194336 | tf_op jit(solution)/shard_map/ppermute | solution.py:14
  909.5 2.3 slice_bitcast_fusion.16
  (973 shorter events, 482.5 us)
Async XLA Ops:
  0.6 9.5 %copy-start.4 = (s32[4,2]{0,1:T(2,128)S(1)}, s32[4,2]{0,1:T(2,128)}, u32[]{:S(2)}) copy-start(s32[4,2]{0,1:T(2,128)} %param.16) | copy-start | bytes 100
  0.6 55.8 %copy-start.1 = (f32[2,128,2048]{2,1,0:T(8,128)S(1)}, f32[2,128,2048]{2,1,0:T(8,128)}, u32[]{:S(2)}) copy-start(f32[2,128,2048]{2,1,0:T(8,128)} %param.14) | copy-start | bytes 6291460
  5.5 51.0 %collective-permute-start.2 = (f32[2,2,128,2048]{3,2,1,0:T(8,128)}, f32[2,2,128,2048]{3,2,1,0:T(8,128)}, u32[]{:S(2)}, u32[]{:S(2)}) collective-permute-start(f32[2,2,128,2048]{3,2,1,0:T(8,128)} %pad_maximum_fusion.3), channel_id=1, source_target_pairs={{0,248},{8,0},{16,8},{24,16},{32,24},{40,32},{48,40},{56,48},{64,5... | collective-permute-start | bytes 12582920 | tf_op jit(solution)/shard_map/ppermute | solution.py:14
  10.1 52.0 %copy-start.3 = (f32[2,128,128]{2,1,0:T(8,128)S(1)}, f32[2,128,128]{2,1,0:T(8,128)}, u32[]{:S(2)}) copy-start(f32[2,128,128]{2,1,0:T(8,128)} %param.15) | copy-start | bytes 393220
  88.2 6.9 collective-permute-start
  121.0 6.9 collective-permute-start
  153.9 6.9 collective-permute-start
  186.8 6.9 collective-permute-start
  219.6 6.9 collective-permute-start
  252.5 7.5 collective-permute-start
  286.0 8.1 collective-permute-start
  320.0 8.4 collective-permute-start
  354.5 8.1 collective-permute-start
  388.7 8.1 collective-permute-start
  422.8 8.1 collective-permute-start
  431.0 5.4 copy-start.2
  472.6 12.8 %collective-permute-start.1 = (f32[1,2,128,128]{3,2,1,0:T(8,128)S(1)}, f32[1,2,128,128]{3,2,1,0:T(8,128)S(1)}, u32[]{:S(2)}, u32[]{:S(2)}) collective-permute-start(f32[1,2,128,128]{3,2,1,0:T(8,128)S(1)} %pad_maximum_fusion.6), channel_id=1, source_target_pairs={{1,0},{2,1},{3,2},{4,3},{5,4},{6,5},{7,6},{9,8},{10,9},{11,10},{12... | collective-permute-start | bytes 393224 | tf_op jit(solution)/shard_map/while/body/eval_jaxpr/ppermute | solution.py:20
  511.0 14.2 %collective-permute-start.1 = (f32[1,2,128,128]{3,2,1,0:T(8,128)S(1)}, f32[1,2,128,128]{3,2,1,0:T(8,128)S(1)}, u32[]{:S(2)}, u32[]{:S(2)}) collective-permute-start(f32[1,2,128,128]{3,2,1,0:T(8,128)S(1)} %pad_maximum_fusion.6), channel_id=1, source_target_pairs={{1,0},{2,1},{3,2},{4,3},{5,4},{6,5},{7,6},{9,8},{10,9},{11,10},{12... | collective-permute-start | bytes 393224 | tf_op jit(solution)/shard_map/while/body/eval_jaxpr/ppermute | solution.py:20
  550.7 12.6 %collective-permute-start.1 = (f32[1,2,128,128]{3,2,1,0:T(8,128)S(1)}, f32[1,2,128,128]{3,2,1,0:T(8,128)S(1)}, u32[]{:S(2)}, u32[]{:S(2)}) collective-permute-start(f32[1,2,128,128]{3,2,1,0:T(8,128)S(1)} %pad_maximum_fusion.6), channel_id=1, source_target_pairs={{1,0},{2,1},{3,2},{4,3},{5,4},{6,5},{7,6},{9,8},{10,9},{11,10},{12... | collective-permute-start | bytes 393224 | tf_op jit(solution)/shard_map/while/body/eval_jaxpr/ppermute | solution.py:20
  588.8 11.1 %collective-permute-start.1 = (f32[1,2,128,128]{3,2,1,0:T(8,128)S(1)}, f32[1,2,128,128]{3,2,1,0:T(8,128)S(1)}, u32[]{:S(2)}, u32[]{:S(2)}) collective-permute-start(f32[1,2,128,128]{3,2,1,0:T(8,128)S(1)} %pad_maximum_fusion.6), channel_id=1, source_target_pairs={{1,0},{2,1},{3,2},{4,3},{5,4},{6,5},{7,6},{9,8},{10,9},{11,10},{12... | collective-permute-start | bytes 393224 | tf_op jit(solution)/shard_map/while/body/eval_jaxpr/ppermute | solution.py:20
  625.4 10.8 %collective-permute-start.1 = (f32[1,2,128,128]{3,2,1,0:T(8,128)S(1)}, f32[1,2,128,128]{3,2,1,0:T(8,128)S(1)}, u32[]{:S(2)}, u32[]{:S(2)}) collective-permute-start(f32[1,2,128,128]{3,2,1,0:T(8,128)S(1)} %pad_maximum_fusion.6), channel_id=1, source_target_pairs={{1,0},{2,1},{3,2},{4,3},{5,4},{6,5},{7,6},{9,8},{10,9},{11,10},{12... | collective-permute-start | bytes 393224 | tf_op jit(solution)/shard_map/while/body/eval_jaxpr/ppermute | solution.py:20
  661.8 10.8 %collective-permute-start.1 = (f32[1,2,128,128]{3,2,1,0:T(8,128)S(1)}, f32[1,2,128,128]{3,2,1,0:T(8,128)S(1)}, u32[]{:S(2)}, u32[]{:S(2)}) collective-permute-start(f32[1,2,128,128]{3,2,1,0:T(8,128)S(1)} %pad_maximum_fusion.6), channel_id=1, source_target_pairs={{1,0},{2,1},{3,2},{4,3},{5,4},{6,5},{7,6},{9,8},{10,9},{11,10},{12... | collective-permute-start | bytes 393224 | tf_op jit(solution)/shard_map/while/body/eval_jaxpr/ppermute | solution.py:20
  698.1 10.8 %collective-permute-start.1 = (f32[1,2,128,128]{3,2,1,0:T(8,128)S(1)}, f32[1,2,128,128]{3,2,1,0:T(8,128)S(1)}, u32[]{:S(2)}, u32[]{:S(2)}) collective-permute-start(f32[1,2,128,128]{3,2,1,0:T(8,128)S(1)} %pad_maximum_fusion.6), channel_id=1, source_target_pairs={{1,0},{2,1},{3,2},{4,3},{5,4},{6,5},{7,6},{9,8},{10,9},{11,10},{12... | collective-permute-start | bytes 393224 | tf_op jit(solution)/shard_map/while/body/eval_jaxpr/ppermute | solution.py:20
  734.5 10.8 %collective-permute-start.1 = (f32[1,2,128,128]{3,2,1,0:T(8,128)S(1)}, f32[1,2,128,128]{3,2,1,0:T(8,128)S(1)}, u32[]{:S(2)}, u32[]{:S(2)}) collective-permute-start(f32[1,2,128,128]{3,2,1,0:T(8,128)S(1)} %pad_maximum_fusion.6), channel_id=1, source_target_pairs={{1,0},{2,1},{3,2},{4,3},{5,4},{6,5},{7,6},{9,8},{10,9},{11,10},{12... | collective-permute-start | bytes 393224 | tf_op jit(solution)/shard_map/while/body/eval_jaxpr/ppermute | solution.py:20
  770.9 10.8 %collective-permute-start.1 = (f32[1,2,128,128]{3,2,1,0:T(8,128)S(1)}, f32[1,2,128,128]{3,2,1,0:T(8,128)S(1)}, u32[]{:S(2)}, u32[]{:S(2)}) collective-permute-start(f32[1,2,128,128]{3,2,1,0:T(8,128)S(1)} %pad_maximum_fusion.6), channel_id=1, source_target_pairs={{1,0},{2,1},{3,2},{4,3},{5,4},{6,5},{7,6},{9,8},{10,9},{11,10},{12... | collective-permute-start | bytes 393224 | tf_op jit(solution)/shard_map/while/body/eval_jaxpr/ppermute | solution.py:20
  807.3 10.8 %collective-permute-start.1 = (f32[1,2,128,128]{3,2,1,0:T(8,128)S(1)}, f32[1,2,128,128]{3,2,1,0:T(8,128)S(1)}, u32[]{:S(2)}, u32[]{:S(2)}) collective-permute-start(f32[1,2,128,128]{3,2,1,0:T(8,128)S(1)} %pad_maximum_fusion.6), channel_id=1, source_target_pairs={{1,0},{2,1},{3,2},{4,3},{5,4},{6,5},{7,6},{9,8},{10,9},{11,10},{12... | collective-permute-start | bytes 393224 | tf_op jit(solution)/shard_map/while/body/eval_jaxpr/ppermute | solution.py:20
  843.6 10.8 %collective-permute-start.1 = (f32[1,2,128,128]{3,2,1,0:T(8,128)S(1)}, f32[1,2,128,128]{3,2,1,0:T(8,128)S(1)}, u32[]{:S(2)}, u32[]{:S(2)}) collective-permute-start(f32[1,2,128,128]{3,2,1,0:T(8,128)S(1)} %pad_maximum_fusion.6), channel_id=1, source_target_pairs={{1,0},{2,1},{3,2},{4,3},{5,4},{6,5},{7,6},{9,8},{10,9},{11,10},{12... | collective-permute-start | bytes 393224 | tf_op jit(solution)/shard_map/while/body/eval_jaxpr/ppermute | solution.py:20
  854.5 53.9 %copy-start = (f32[2,2,256,2048]{3,2,0,1:T(8,128)S(1)}, f32[2,2,256,2048]{3,2,0,1:T(8,128)}, u32[]{:S(2)}) copy-start(f32[2,2,256,2048]{3,2,0,1:T(8,128)} %get-tuple-element.563) | copy-start | bytes 25165828
  857.1 51.3 %collective-permute-start.3 = (f32[2,2,128,2048]{3,2,0,1:T(8,128)S(1)}, f32[2,2,128,2048]{3,2,0,1:T(8,128)S(1)}, u32[]{:S(2)}, u32[]{:S(2)}) collective-permute-start(f32[2,2,128,2048]{3,2,0,1:T(8,128)S(1)} %slice.128), channel_id=1, source_target_pairs={{0,8},{8,16},{16,24},{24,32},{32,40},{40,48},{48,56},{56,64},{64,7... | collective-permute-start | bytes 12582920 | tf_op jit(solution)/shard_map/ppermute | solution.py:14
where the time goes:
time: 930 us; the launch traced here: 912 us
  matrix products  409 us (44%)
  waiting for transfers between devices  163 us (18%)
  loops' own time  142 us (15%)
  local copies, waits for them, and re-layouts  122 us (13%)
  starting transfers between devices  48.4 us (5%)
  other arithmetic  26.3 us (3%)
    dot_general x360, matrix products, left_times(): jnp.einsum('jk,...kl->...jl', matrix, field, precision=lax.Precision.HIGH...  240 us
    dot_general x360, matrix products, right_times(): jnp.einsum('...jk,kl->...jl', field, matrix, precision=lax.Precision.HIGH...  169 us
    ppermute x2, waiting for transfers between devices, shifted(): return lax.ppermute(value, axis, pairs)  97.5 us
    another operation x1, loops' own time, shards(): lax.scan(backward_step, back_state, jnp.arange(step_count))  89.4 us
    ppermute x22, waiting for transfers between devices, from_behind(): return lax.ppermute(shard, axis, pairs)  65.9 us
    another operation x1, loops' own time, shards(): lax.scan(forward_step, start_state, jnp.arange(step_count))  52.2 us
    ppermute x22, starting transfers between devices, from_behind(): return lax.ppermute(shard, axis, pairs)  43.7 us
    dynamic_update_slice x22, local copies, waits for them, and re-layouts, add_one(): lax.dynamic_update_slice(total, region + contrib[member], (0, 0, row_at,...  43.5 us
  transfers between devices with their start and end apart: 24, of which 13 were waited for; matrix products, arithmetic and copies ran while one was open for 6% of the time, Pallas kernels for 0%

commit v1 on v0

v1 whole, which is shorter than its diff:
```python
import functools
import math

import jax
import jax.numpy as jnp
import ml_dtypes
import numpy as np
from jax import lax
from jax.experimental import pallas as pl
from jax.experimental.pallas import tpu as pltpu
from jax.sharding import PartitionSpec as P

f32, bf16 = jnp.float32, jnp.bfloat16
phase_scale = 32.0
TILE, CUTS = "tile", "cuts"
RIGHT_A, RIGHT_A_CONJ, RIGHT_F, RIGHT_F_CONJ = range(4)


def tables(n):
    index = np.arange(n)
    dft = np.exp(-2j * np.pi * (np.outer(index, index) % n) / n) / math.sqrt(n)
    freq = np.where(index < n // 2, index, index - n).astype(np.float64)
    turn = np.exp(-1j * phase_scale * freq**2 / (n * n))
    step = np.conj(dft) @ (turn[:, None] * dft)

    def parts(matrix):
        block = np.block([[matrix.real, matrix.imag], [-matrix.imag, matrix.real]])
        high = block.astype(ml_dtypes.bfloat16)
        low = (block - high.astype(np.float64)).astype(ml_dtypes.bfloat16)
        rest = (block - high.astype(np.float64) - low.astype(np.float64)).astype(ml_dtypes.bfloat16)
        return high, low, rest

    rights, lefts = [], []
    for matrix in (step, step.conj(), dft, dft.conj()):
        high, low, rest = parts(matrix)
        rights.append(np.concatenate([high, high, low, rest], 0))
        lefts.append(np.concatenate([high.T, low.T, rest.T], 1))
    return np.stack(rights), np.stack(lefts)


def split(value):
    high = value.astype(bf16)
    return high, (value - high.astype(f32)).astype(bf16)


def dot(a, b):
    return jnp.dot(a, b, preferred_element_type=f32)


def right_times(re, im, table):
    n = re.shape[1]
    high, low = split(jnp.concatenate([re, im], 1))
    out = dot(jnp.concatenate([high, low, high, high], 1), table[...])
    return out[:, :n], out[:, n:]


def left_times(re, im, table):
    n = re.shape[0]
    high, low = split(jnp.concatenate([re, im], 0))
    main = dot(table[:, : 2 * n], jnp.concatenate([high, low], 1))
    rest = dot(table[:, 2 * n :], jnp.concatenate([high, high], 0))
    out = main[:, :n] + main[:, n:] + rest
    return out[:n], out[n:]


def both_sides(re, im, rights, lefts, which):
    re, im = right_times(re, im, rights.at[which])
    return left_times(re, im, lefts.at[which])


def wave_kernel(patch_at, probe, counts, rights, lefts, out, psi):
    count = psi.shape[0]

    psi[0] = probe[...]

    def forward(s, carry):
        a, b = psi[s, 0], psi[s, 1]
        p, q = patch_at(s)
        re, im = both_sides(p * a - q * b, p * b + q * a, rights, lefts, RIGHT_A)
        psi[s + 1, 0] = re
        psi[s + 1, 1] = im
        return carry

    lax.fori_loop(0, count - 1, forward, 0)
    a, b = psi[count - 1, 0], psi[count - 1, 1]
    p, q = patch_at(count - 1)
    re, im = both_sides(p * a - q * b, p * b + q * a, rights, lefts, RIGHT_F)
    weight = 4.0 * (re * re + im * im - counts.astype(f32))
    re, im = both_sides(weight * re, weight * im, rights, lefts, RIGHT_F_CONJ)

    def put(s, re, im):
        a, b = psi[s, 0], psi[s, 1]
        out[s, 0] = a * re + b * im
        out[s, 1] = a * im - b * re

    put(count - 1, re, im)

    def backward(i, carry):
        re, im = carry
        s = count - 1 - i
        p, q = patch_at(s)
        re, im = both_sides(p * re + q * im, p * im - q * re, rights, lefts, RIGHT_A_CONJ)
        put(s - 1, re, im)
        return re, im

    lax.fori_loop(0, count - 1, backward, (re, im))


def take_kernel(meta, real0, real1, imag0, imag1, probe, win, rolled):
    w = pl.program_id(0)
    n = probe.shape[1]
    shape = (n, n)
    rows = lax.broadcasted_iota(jnp.int32, shape, 0)
    cols = lax.broadcasted_iota(jnp.int32, shape, 1)
    split_row, split_col = meta[1, w], meta[2, w]
    own = w < pl.num_programs(0) // 2
    keep = jnp.where(own, (rows >= split_row).astype(jnp.int32), (rows < split_row).astype(jnp.int32)) > 0
    first = cols >= split_col
    for s in range(real0.shape[0]):
        win[0, s, 0] = jnp.where(keep, jnp.where(first, real0[s], real1[s]), 0.0)
        win[0, s, 1] = jnp.where(keep, jnp.where(first, imag0[s], imag1[s]), 0.0)

    @pl.when(w == 0)
    def _():
        at = meta.shape[1] - 1
        for i in range(2):
            turned = pltpu.roll(probe[i], meta[1, at], 0)
            rolled[i] = pltpu.roll(turned, meta[2, at], 1)


def take(meta, object_real, object_imag, probe):
    slices, rows, cols = object_real.shape
    n = probe.shape[1]
    count = meta.shape[1] - 1
    last = cols // n - 1
    block = lambda index: pl.BlockSpec((slices, n, n), index)
    here = lambda w, meta: (0, 0, meta[0, w])
    beside = lambda w, meta: (0, 0, jnp.minimum(meta[0, w] + 1, last))
    return pl.pallas_call(
        take_kernel,
        out_shape=(
            jax.ShapeDtypeStruct((count, slices, 2, n, n), f32),
            jax.ShapeDtypeStruct((2, n, n), f32),
        ),
        grid_spec=pltpu.PrefetchScalarGridSpec(
            num_scalar_prefetch=1,
            grid=(count,),
            in_specs=[
                block(here),
                block(beside),
                block(here),
                block(beside),
                pl.BlockSpec((2, n, n), lambda w, meta: (0, 0, 0)),
            ],
            out_specs=(
                pl.BlockSpec((1, slices, 2, n, n), lambda w, meta: (w, 0, 0, 0, 0)),
                pl.BlockSpec((2, n, n), lambda w, meta: (0, 0, 0)),
            ),
        ),
    )(meta, object_real, object_real, object_imag, object_imag, probe)


def add_kernel(meta, own, other, real, imag):
    n = own.shape[-1]
    count = own.shape[0]
    shape = (n, n)
    rows = lax.broadcasted_iota(jnp.int32, shape, 0)
    cols = lax.broadcasted_iota(jnp.int32, shape, 1)
    last = real.shape[2] // n - 1
    real[...] = jnp.zeros_like(real)
    imag[...] = jnp.zeros_like(imag)
    for w in range(2 * count):
        source = own.at[w] if w < count else other.at[w - count]
        block, split_row, split_col = meta[0, w], meta[1, w], meta[2, w]
        keep = (rows >= split_row) if w < count else (rows < split_row)
        here = pl.ds(pl.multiple_of(block * n, n), n)
        beside = pl.ds(pl.multiple_of(jnp.minimum(block + 1, last) * n, n), n)
        first = cols >= split_col
        for i, target in enumerate((real, imag)):
            value = jnp.where(keep, source[0, i], 0.0)
            target[0, :, here] += jnp.where(first, value, 0.0)
            target[0, :, beside] += jnp.where(first, 0.0, value)


def add(meta, own, other, shape):
    slices, rows, cols = shape
    count, _, _, n, _ = own.shape
    window = pl.BlockSpec((count, 1, 2, n, n), lambda s, meta: (0, s, 0, 0, 0))
    strip = pl.BlockSpec((1, rows, cols), lambda s, meta: (s, 0, 0))
    return pl.pallas_call(
        add_kernel,
        out_shape=(jax.ShapeDtypeStruct(shape, f32),) * 2,
        grid_spec=pltpu.PrefetchScalarGridSpec(
            num_scalar_prefetch=1,
            grid=(slices,),
            in_specs=[window, window],
            out_specs=(strip, strip),
        ),
        compiler_params=pltpu.CompilerParams(vmem_limit_bytes=32 << 20),
    )(meta, own, other)


def plain_kernel(patches, probe, counts, rights, lefts, out, psi):
    me = lax.axis_index(CUTS)
    cuts, slices = patches.shape[:2]

    def patch_at(s):
        at, inner = lax.rem(me - s // slices + cuts, cuts), lax.rem(s, slices)
        return patches[at, inner, 0], patches[at, inner, 1]

    wave_kernel(patch_at, probe, counts[...], rights, lefts, out, psi)


def shards(object_real, object_imag, probe, positions, counts):
    cuts, tiles = lax.axis_size(CUTS), lax.axis_size(TILE)
    me, tile = lax.axis_index(CUTS), lax.axis_index(TILE)
    slices, rows, cols = object_real.shape
    n = probe.shape[1]
    count = positions.shape[0]
    spread = cuts // count
    phase = lax.rem(tile, spread)
    back = [(t, (t - 1) % tiles) for t in range(tiles)]
    ahead = [(t, (t + 1) % tiles) for t in range(tiles)]

    def places(position):
        return jnp.stack([position[:, 1] // n, position[:, 0] % n, position[:, 1] % n])

    own_places = places(positions)
    other_places = lax.ppermute(own_places, TILE, ahead)
    held = lax.div(me + cuts - phase, spread) % count
    mine = lax.dynamic_slice_in_dim(own_places, held, 1, 1)
    meta = jnp.concatenate([own_places, other_places, mine], 1)
    windows, rolled = take(meta, object_real, object_imag, probe)
    merged = windows[:count] + lax.ppermute(windows[count:], TILE, back)

    def owner(k, t):
        return (k * spread + t % spread) % cuts

    def pairs(d):
        out = []
        for t in range(tiles):
            for k in range(count):
                o = owner(k, t)
                out.append((t * cuts + (o - d) % cuts, t * cuts + o))
        return out

    got = []
    for d in range(cuts):
        k = lax.div(lax.rem(me + d + cuts - phase, cuts), spread)
        piece = lax.dynamic_index_in_dim(merged, k, 0, False)
        got.append(piece if d == 0 else lax.ppermute(piece, (TILE, CUTS), pairs(d)))
    patches = jnp.stack(got)
    rights, lefts = (jnp.asarray(t) for t in tables(n))
    contrib = pl.pallas_call(
        plain_kernel,
        out_shape=jax.ShapeDtypeStruct((cuts * slices, 2, n, n), f32),
        in_specs=[pl.BlockSpec(memory_space=pltpu.VMEM)] * 5,
        out_specs=pl.BlockSpec(memory_space=pltpu.VMEM),
        scratch_shapes=[pltpu.VMEM((cuts * slices, 2, n, n), f32)],
        compiler_params=pltpu.CompilerParams(vmem_limit_bytes=40 << 20),
    )(patches, rolled, lax.dynamic_index_in_dim(counts, held, 0, False), rights, lefts)
    contrib = contrib.reshape(cuts, slices, 2, n, n)
    is_owner = lax.rem(me + cuts - phase, spread) == 0
    sums = [0.0] * count
    for d in range(cuts):
        piece = lax.dynamic_index_in_dim(contrib, lax.rem(me - d + cuts, cuts), 0, False)
        if d == 0:
            piece = jnp.where(is_owner, piece, 0.0)
        else:
            piece = lax.ppermute(piece, (TILE, CUTS), [(b, a) for a, b in pairs(d)])
        sums[d // spread] = sums[d // spread] + piece
    own = jnp.stack(sums)
    order = []
    lag = lax.rem(phase - me + cuts, spread)
    for j in range(count):
        o = lax.rem(me + j * spread + lag, cuts)
        order.append(lax.div(lax.rem(o - phase + cuts, cuts), spread))
    picked = own_places[:, jnp.stack(order)]
    other = lax.ppermute(own, TILE, ahead)
    meta = jnp.concatenate([picked, lax.ppermute(picked, TILE, ahead)], 1)
    return add(meta, own, other, object_real.shape)


def solution(mesh):
    placed = (
        P("cuts", "tile", None),
        P("cuts", "tile", None),
        P(),
        P("tile", None),
        P("tile", None, None),
    )
    return jax.shard_map(
        shards,
        mesh=mesh,
        in_specs=placed,
        out_specs=(P("cuts", "tile", None), P("cuts", "tile", None)),
        check_vma=False,
    )
```

time: 930 us -> 149 us (0.16)
  the two profiles are of different devices: /device:TPU:224 before, /device:TPU:0 now
where the time goes in v1:
time: 149 us; the launch traced here: 148 us
  waiting for transfers between devices  65.6 us (44%)
  starting transfers between devices  40.9 us (27%)
  Pallas kernels  27.9 us (19%)
  local copies, waits for them, and re-layouts  10.6 us (7%)
  other arithmetic  1.92 us (1%)
    ppermute x7, starting transfers between devices, shards(): got.append(piece if d == 0 else lax.ppermute(piece, (TILE, CUTS), pairs(d)))  20.6 us
    ppermute x7, waiting for transfers between devices, shards(): piece = lax.ppermute(piece, (TILE, CUTS), [(b, a) for a, b in pairs(d)])  20.5 us
    ppermute x7, starting transfers between devices, shards(): piece = lax.ppermute(piece, (TILE, CUTS), [(b, a) for a, b in pairs(d)])  20.1 us
    pallas_call x1, Pallas kernels, shards(): pl.pallas_call(plain_kernel, out_shape=jax.ShapeDtypeStruct((cuts * slice...  17.5 us
    ppermute x1, waiting for transfers between devices, shards(): meta = jnp.concatenate([picked, lax.ppermute(picked, TILE, ahead)], 1)  16.7 us
    ppermute x1, waiting for transfers between devices, shards(): merged = windows[:count] + lax.ppermute(windows[count:], TILE, back)  12.6 us
    ppermute x7, waiting for transfers between devices, shards(): got.append(piece if d == 0 else lax.ppermute(piece, (TILE, CUTS), pairs(d)))  9.56 us
    pallas_call x1, Pallas kernels, take(): pl.pallas_call(take_kernel, out_shape=(jax.ShapeDtypeStruct((count, slice...  7.19 us
  transfers between devices with their start and end apart: 18, of which 10 were waited for; matrix products, arithmetic and copies ran while one was open for 2% of the time, Pallas kernels for 0%

profile of v1, /device:TPU:0, one launch (start us, length us, event | category | flops | bytes accessed | tf_op | source)
XLA Modules:
  0.0 147.9 jit_solution(16356400366280593178)
XLA Ops:
  0.6 0.0 copy-start
  0.6 0.8 and_select_fusion.2
  1.4 0.1 collective-permute-start.1
  1.6 0.1 constant_dynamic-slice_fusion
  1.6 6.2 %collective-permute-done.1 = s32[3,4]{1,0:T(4,128)S(1)} collective-permute-done((s32[3,4]{1,0:T(4,128)S(1)}, s32[3,4]{1,0:T(4,128)S(1)}, u32[]{:S(2)}, u32[]{:S(2)}) %collective-permute-start.1) | collective-permute-done | bytes 80 | tf_op jit(solution)/shard_map/ppermute | solution.py:229
  7.8 0.7 pad_add_fusion.2.meta
  8.5 7.2 %shard_map.86 = (f32[8,2,2,128,128]{4,3,2,1,0:T(8,128)}, f32[2,128,128]{2,1,0:T(8,128)}) custom-call(s32[3,9]{1,0:T(4,128)} %pad_add_fusion.2.meta, f32[2,128,2048]{2,1,0:T(8,128)} %real1.1, f32[2,128,2048]{2,1,0:T(8,128)} %real1.1, f32[2,128,2048]{2,1,0:T(8,128)} %imag1.1, f32[2,128,2048]{2,1,0:T(8,128)} %imag1.1, f32[2,128,128]{2,1,0:T(8,128)} %probe.1), custom_call_target="tpu_custom_call" | custom-call | tf_op jit(solution)/shard_map/pallas_call | solution.py:139
  15.7 2.4 %slice.16 = f32[4,2,2,128,128]{4,3,2,1,0:T(8,128)} slice(f32[8,2,2,128,128]{4,3,2,1,0:T(8,128)} %get-tuple-element.4), slice={[4:8], [0:2], [0:2], [0:128], [0:128]} | slice | bytes 2097152 | tf_op jit(solution)/shard_map/slice | solution.py:234
  18.1 0.0 collective-permute-start.2
  18.1 12.6 %collective-permute-done.2 = f32[4,2,2,128,128]{4,3,2,1,0:T(8,128)S(1)} collective-permute-done((f32[4,2,2,128,128]{4,3,2,1,0:T(8,128)}, f32[4,2,2,128,128]{4,3,2,1,0:T(8,128)S(1)}, u32[]{:S(2)}, u32[]{:S(2)}) %collective-permute-start.2) | collective-permute-done | bytes 1048608 | tf_op jit(solution)/shard_map/ppermute | solution.py:234
  30.8 0.0 copy-done.6
  30.8 0.1 slice_add_fusion
  30.9 1.1 dynamic-slice_bitcast_fusion.7
  32.0 1.4 collective-permute-start.3
  33.4 3.4 %collective-permute-start.4 = (f32[2,2,128,128]{3,2,1,0:T(8,128)}, f32[2,2,128,128]{3,2,1,0:T(8,128)}, u32[]{:S(2)}, u32[]{:S(2)}) collective-permute-start(f32[2,2,128,128]{3,2,1,0:T(8,128)} %get-tuple-element.20), channel_id=1, source_target_pairs={{6,0},{0,2},{2,4},{4,6},{15,9},{9,11},{11,13},{13,15},{22,16},{16,... | collective-permute-start | bytes 786440 | tf_op jit(solution)/shard_map/ppermute | solution.py:251
  36.9 0.0 copy-done
  36.9 0.0 copy-start.3
  36.9 0.0 copy-start.4
  37.0 1.6 %collective-permute-start.9 = (f32[2,2,128,128]{3,2,1,0:T(8,128)S(1)}, f32[2,2,128,128]{3,2,1,0:T(8,128)S(1)}, u32[]{:S(2)}, u32[]{:S(2)}) collective-permute-start(f32[2,2,128,128]{3,2,1,0:T(8,128)S(1)} %get-tuple-element.15), channel_id=1, source_target_pairs={{1,0},{3,2},{5,4},{7,6},{10,9},{12,11},{14,13},{8,15},{17,16},{19,... | collective-permute-start | bytes 786440 | tf_op jit(solution)/shard_map/ppermute | solution.py:251
  38.5 5.0 %collective-permute-start.8 = (f32[2,2,128,128]{3,2,1,0:T(8,128)S(1)}, f32[2,2,128,128]{3,2,1,0:T(8,128)S(1)}, u32[]{:S(2)}, u32[]{:S(2)}) collective-permute-start(f32[2,2,128,128]{3,2,1,0:T(8,128)S(1)} %get-tuple-element.16), channel_id=1, source_target_pairs={{2,0},{4,2},{6,4},{0,6},{11,9},{13,11},{15,13},{9,15},{18,16},{20,... | collective-permute-start | bytes 786440 | tf_op jit(solution)/shard_map/ppermute | solution.py:251
  43.5 1.3 collective-permute-start.7
  44.8 2.7 %collective-permute-done.3 = f32[2,2,128,128]{3,2,1,0:T(8,128)} collective-permute-done((f32[2,2,128,128]{3,2,1,0:T(8,128)}, f32[2,2,128,128]{3,2,1,0:T(8,128)}, u32[]{:S(2)}, u32[]{:S(2)}) %collective-permute-start.3) | collective-permute-done | bytes 262176 | tf_op jit(solution)/shard_map/ppermute | solution.py:251
  47.4 1.3 collective-permute-start.5
  48.7 1.0 bitcast_dynamic-update-slice_fusion.6
  49.7 0.0 collective-permute-done.4
  49.7 6.6 %collective-permute-start.6 = (f32[2,2,128,128]{3,2,1,0:T(8,128)}, f32[2,2,128,128]{3,2,1,0:T(8,128)S(1)}, u32[]{:S(2)}, u32[]{:S(2)}) collective-permute-start(f32[2,2,128,128]{3,2,1,0:T(8,128)} %get-tuple-element.18), channel_id=1, source_target_pairs={{4,0},{6,2},{0,4},{2,6},{13,9},{15,11},{9,13},{11,15},{20,16},{22,... | collective-permute-start | bytes 786440 | tf_op jit(solution)/shard_map/ppermute | solution.py:251
  56.4 1.0 bitcast_dynamic-update-slice_fusion.5
  57.3 2.6 %collective-permute-done.5 = f32[2,2,128,128]{3,2,1,0:T(8,128)S(1)} collective-permute-done((f32[2,2,128,128]{3,2,1,0:T(8,128)}, f32[2,2,128,128]{3,2,1,0:T(8,128)S(1)}, u32[]{:S(2)}, u32[]{:S(2)}) %collective-permute-start.5) | collective-permute-done | bytes 262176 | tf_op jit(solution)/shard_map/ppermute | solution.py:251
  59.9 4.3 %collective-permute-done.6 = f32[2,2,128,128]{3,2,1,0:T(8,128)S(1)} collective-permute-done((f32[2,2,128,128]{3,2,1,0:T(8,128)}, f32[2,2,128,128]{3,2,1,0:T(8,128)S(1)}, u32[]{:S(2)}, u32[]{:S(2)}) %collective-permute-start.6) | collective-permute-done | bytes 262176 | tf_op jit(solution)/shard_map/ppermute | solution.py:251
  64.3 0.0 collective-permute-done.7
  64.3 0.0 collective-permute-done.8
  64.3 0.0 collective-permute-done.9
  64.4 0.0 copy-start.1
  64.4 1.3 copy-done.1
  65.7 0.0 copy-done.5
  65.7 0.0 copy-done.3
  65.7 1.6 %copy-done.2 = f32[8,2,2,128,128]{4,3,2,1,0:T(8,128)S(1)} copy-done((f32[8,2,2,128,128]{4,3,2,1,0:T(8,128)S(1)}, f32[8,2,2,128,128]{4,3,2,1,0:T(8,128)}, u32[]{:S(2)}) %copy-start.2) | copy-done | bytes 2097176
  67.3 17.5 %shard_map.87 = f32[16,2,128,128]{3,2,1,0:T(8,128)S(1)} custom-call(f32[8,2,2,128,128]{4,3,2,1,0:T(8,128)S(1)} %copy-done.2, f32[2,128,128]{2,1,0:T(8,128)S(1)} %copy-done.5, s32[128,128]{1,0:T(8,128)S(1)} %dynamic-slice_bitcast_fusion.14.counts, bf16[4,1024,256]{2,1,0:T(8,128)(2,1)S(1)} %copy-done.3, bf16[4,256,768]{2,1,0:T(8,128)(2,1)S(1)} %copy-done.4), custom_call_target="tpu_custom_call" | custom-call | tf_op jit(solution)/shard_map/pallas_call | solution.py:254
  84.8 1.3 dynamic-slice_bitcast_fusion.6
  86.0 1.6 %collective-permute-start.16 = (f32[2,2,128,128]{3,2,1,0:T(8,128)}, f32[2,2,128,128]{3,2,1,0:T(8,128)S(1)}, u32[]{:S(2)}, u32[]{:S(2)}) collective-permute-start(f32[2,2,128,128]{3,2,1,0:T(8,128)} %get-tuple-element.9), channel_id=1, source_target_pairs={{0,1},{2,3},{4,5},{6,7},{9,10},{11,12},{13,14},{15,8},{16,17},{18,... | collective-permute-start | bytes 786440 | tf_op jit(solution)/shard_map/ppermute | solution.py:270
  87.7 7.7 %collective-permute-start.15 = (f32[2,2,128,128]{3,2,1,0:T(8,128)}, f32[2,2,128,128]{3,2,1,0:T(8,128)S(1)}, u32[]{:S(2)}, u32[]{:S(2)}) collective-permute-start(f32[2,2,128,128]{3,2,1,0:T(8,128)} %get-tuple-element.10), channel_id=1, source_target_pairs={{0,2},{2,4},{4,6},{6,0},{9,11},{11,13},{13,15},{15,9},{16,18},{18,... | collective-permute-start | bytes 786440 | tf_op jit(solution)/shard_map/ppermute | solution.py:270
  95.4 1.3 collective-permute-start.14
  96.7 5.0 %collective-permute-start.13 = (f32[2,2,128,128]{3,2,1,0:T(8,128)}, f32[2,2,128,128]{3,2,1,0:T(8,128)S(1)}, u32[]{:S(2)}, u32[]{:S(2)}) collective-permute-start(f32[2,2,128,128]{3,2,1,0:T(8,128)} %get-tuple-element.12), channel_id=1, source_target_pairs={{0,4},{2,6},{4,0},{6,2},{9,13},{11,15},{13,9},{15,11},{16,20},{18,... | collective-permute-start | bytes 786440 | tf_op jit(solution)/shard_map/ppermute | solution.py:270
  101.7 1.3 collective-permute-start.10
  103.0 0.0 collective-permute-done.16
  103.0 1.3 collective-permute-start.12
  104.3 2.8 %collective-permute-done.15 = f32[2,2,128,128]{3,2,1,0:T(8,128)S(1)} collective-permute-done((f32[2,2,128,128]{3,2,1,0:T(8,128)}, f32[2,2,128,128]{3,2,1,0:T(8,128)S(1)}, u32[]{:S(2)}, u32[]{:S(2)}) %collective-permute-start.15) | collective-permute-done | bytes 262176 | tf_op jit(solution)/shard_map/ppermute | solution.py:270
  107.1 1.9 %collective-permute-start.11 = (f32[2,2,128,128]{3,2,1,0:T(8,128)}, f32[2,2,128,128]{3,2,1,0:T(8,128)S(1)}, u32[]{:S(2)}, u32[]{:S(2)}) collective-permute-start(f32[2,2,128,128]{3,2,1,0:T(8,128)} %get-tuple-element.14), channel_id=1, source_target_pairs={{0,6},{2,0},{4,2},{6,4},{9,15},{11,9},{13,11},{15,13},{16,22},{18,... | collective-permute-start | bytes 786440 | tf_op jit(solution)/shard_map/ppermute | solution.py:270
  109.1 0.0 collective-permute-done.14
  109.1 7.0 %collective-permute-done.13 = f32[2,2,128,128]{3,2,1,0:T(8,128)S(1)} collective-permute-done((f32[2,2,128,128]{3,2,1,0:T(8,128)}, f32[2,2,128,128]{3,2,1,0:T(8,128)S(1)}, u32[]{:S(2)}, u32[]{:S(2)}) %collective-permute-start.13) | collective-permute-done | bytes 262176 | tf_op jit(solution)/shard_map/ppermute | solution.py:270
  116.2 5.1 %collective-permute-done.12 = f32[2,2,128,128]{3,2,1,0:T(8,128)S(1)} collective-permute-done((f32[2,2,128,128]{3,2,1,0:T(8,128)}, f32[2,2,128,128]{3,2,1,0:T(8,128)S(1)}, u32[]{:S(2)}, u32[]{:S(2)}) %collective-permute-start.12) | collective-permute-done | bytes 262176 | tf_op jit(solution)/shard_map/ppermute | solution.py:270
  121.2 5.6 %collective-permute-done.11 = f32[2,2,128,128]{3,2,1,0:T(8,128)S(1)} collective-permute-done((f32[2,2,128,128]{3,2,1,0:T(8,128)}, f32[2,2,128,128]{3,2,1,0:T(8,128)S(1)}, u32[]{:S(2)}, u32[]{:S(2)}) %collective-permute-start.11) | collective-permute-done | bytes 262176 | tf_op jit(solution)/shard_map/ppermute | solution.py:270
  126.8 0.0 collective-permute-done.10
  126.9 0.1 pad_maximum_fusion.own
  127.0 0.1 collective-permute-start.17
  127.1 0.1 copy.9
  127.2 0.1 fusion.2
  127.3 0.6 gather_fusion
  127.8 0.1 copy.10
  127.9 0.0 collective-permute-start
  127.9 16.7 %collective-permute-done = s32[3,4]{1,0:T(4,128)S(1)} collective-permute-done((s32[3,4]{1,0:T(4,128)S(1)}, s32[3,4]{1,0:T(4,128)S(1)}, u32[]{:S(2)}, u32[]{:S(2)}) %collective-permute-start) | collective-permute-done | bytes 80 | tf_op jit(solution)/shard_map/ppermute | solution.py:280
  144.6 0.1 pad_add_fusion.1.meta
  144.7 0.0 collective-permute-done.17.other
  144.7 3.2 %shard_map.88 = (f32[2,128,2048]{2,1,0:T(8,128)}, f32[2,128,2048]{2,1,0:T(8,128)}) custom-call(s32[3,8]{1,0:T(4,128)S(1)} %pad_add_fusion.1.meta, f32[4,2,2,128,128]{4,3,2,1,0:T(8,128)S(1)} %pad_maximum_fusion.own, f32[4,2,2,128,128]{4,3,2,1,0:T(8,128)S(1)} %collective-permute-done.17.other), custom_call_target="tpu_custom_call" | custom-call | tf_op jit(solution)/shard_map/pallas_call | solution.py:190
  (17 shorter events, 0.3 us)
Async XLA Ops:
  0.6 36.2 %copy-start = (s32[4,128,128]{2,1,0:T(8,128)S(1)}, s32[4,128,128]{2,1,0:T(8,128)}, u32[]{:S(2)}) copy-start(s32[4,128,128]{2,1,0:T(8,128)} %param.11) | copy-start | bytes 786436
  1.4 6.4 %collective-permute-start.1 = (s32[3,4]{1,0:T(4,128)S(1)}, s32[3,4]{1,0:T(4,128)S(1)}, u32[]{:S(2)}, u32[]{:S(2)}) collective-permute-start(s32[3,4]{1,0:T(4,128)S(1)} %pad_add_fusion), channel_id=1, source_target_pairs={{0,8},{8,16},{16,24},{24,32},{32,40},{40,48},{48,56},{56,64},{64,7... | collective-permute-start | bytes 152 | tf_op jit(solution)/shard_map/ppermute | solution.py:229
  15.7 15.1 %copy-start.6 = (f32[8,2,2,128,128]{4,3,2,1,0:T(8,128)S(1)}, f32[8,2,2,128,128]{4,3,2,1,0:T(8,128)}, u32[]{:S(2)}) copy-start(f32[8,2,2,128,128]{4,3,2,1,0:T(8,128)} %get-tuple-element.4) | copy-start | bytes 6291460
  18.1 12.6 %collective-permute-start.2 = (f32[4,2,2,128,128]{4,3,2,1,0:T(8,128)}, f32[4,2,2,128,128]{4,3,2,1,0:T(8,128)S(1)}, u32[]{:S(2)}, u32[]{:S(2)}) collective-permute-start(f32[4,2,2,128,128]{4,3,2,1,0:T(8,128)} %slice.16), channel_id=1, source_target_pairs={{0,248},{8,0},{16,8},{24,16},{32,24},{40,32},{48,40},{56,48},{64,5... | collective-permute-start | bytes 3145736 | tf_op jit(solution)/shard_map/ppermute | solution.py:234
  32.0 33.7 %copy-start.5 = (f32[2,128,128]{2,1,0:T(8,128)S(1)}, f32[2,128,128]{2,1,0:T(8,128)}, u32[]{:S(2)}) copy-start(f32[2,128,128]{2,1,0:T(8,128)} %get-tuple-element.5.probe) | copy-start | bytes 393220
  32.0 15.5 %collective-permute-start.3 = (f32[2,2,128,128]{3,2,1,0:T(8,128)}, f32[2,2,128,128]{3,2,1,0:T(8,128)}, u32[]{:S(2)}, u32[]{:S(2)}) collective-permute-start(f32[2,2,128,128]{3,2,1,0:T(8,128)} %get-tuple-element.21), channel_id=1, source_target_pairs={{7,0},{1,2},{3,4},{5,6},{8,9},{10,11},{12,13},{14,15},{23,16},{17,... | collective-permute-start | bytes 786440 | tf_op jit(solution)/shard_map/ppermute | solution.py:251
  33.4 16.3 %collective-permute-start.4 = (f32[2,2,128,128]{3,2,1,0:T(8,128)}, f32[2,2,128,128]{3,2,1,0:T(8,128)}, u32[]{:S(2)}, u32[]{:S(2)}) collective-permute-start(f32[2,2,128,128]{3,2,1,0:T(8,128)} %get-tuple-element.20), channel_id=1, source_target_pairs={{6,0},{0,2},{2,4},{4,6},{15,9},{9,11},{11,13},{13,15},{22,16},{16,... | collective-permute-start | bytes 786440 | tf_op jit(solution)/shard_map/ppermute | solution.py:251
  36.9 28.8 %copy-start.3 = (bf16[4,1024,256]{2,1,0:T(8,128)(2,1)S(1)}, bf16[4,1024,256]{2,1,0:T(8,128)(2,1)}, u32[]{:S(2)}) copy-start(bf16[4,1024,256]{2,1,0:T(8,128)(2,1)} %constant.222.clone.rights) | copy-start | bytes 6291460
  36.9 28.8 %copy-start.4 = (bf16[4,256,768]{2,1,0:T(8,128)(2,1)S(1)}, bf16[4,256,768]{2,1,0:T(8,128)(2,1)}, u32[]{:S(2)}) copy-start(bf16[4,256,768]{2,1,0:T(8,128)(2,1)} %constant.223.clone.lefts) | copy-start | bytes 4718596
  37.0 27.4 %collective-permute-start.9 = (f32[2,2,128,128]{3,2,1,0:T(8,128)S(1)}, f32[2,2,128,128]{3,2,1,0:T(8,128)S(1)}, u32[]{:S(2)}, u32[]{:S(2)}) collective-permute-start(f32[2,2,128,128]{3,2,1,0:T(8,128)S(1)} %get-tuple-element.15), channel_id=1, source_target_pairs={{1,0},{3,2},{5,4},{7,6},{10,9},{12,11},{14,13},{8,15},{17,16},{19,... | collective-permute-start | bytes 786440 | tf_op jit(solution)/shard_map/ppermute | solution.py:251
  38.5 25.8 %collective-permute-start.8 = (f32[2,2,128,128]{3,2,1,0:T(8,128)S(1)}, f32[2,2,128,128]{3,2,1,0:T(8,128)S(1)}, u32[]{:S(2)}, u32[]{:S(2)}) collective-permute-start(f32[2,2,128,128]{3,2,1,0:T(8,128)S(1)} %get-tuple-element.16), channel_id=1, source_target_pairs={{2,0},{4,2},{6,4},{0,6},{11,9},{13,11},{15,13},{9,15},{18,16},{20,... | collective-permute-start | bytes 786440 | tf_op jit(solution)/shard_map/ppermute | solution.py:251
  43.5 20.8 %collective-permute-start.7 = (f32[2,2,128,128]{3,2,1,0:T(8,128)S(1)}, f32[2,2,128,128]{3,2,1,0:T(8,128)S(1)}, u32[]{:S(2)}, u32[]{:S(2)}) collective-permute-start(f32[2,2,128,128]{3,2,1,0:T(8,128)S(1)} %get-tuple-element.17), channel_id=1, source_target_pairs={{3,0},{5,2},{7,4},{1,6},{12,9},{14,11},{8,13},{10,15},{19,16},{21,... | collective-permute-start | bytes 786440 | tf_op jit(solution)/shard_map/ppermute | solution.py:251
  47.4 12.5 %collective-permute-start.5 = (f32[2,2,128,128]{3,2,1,0:T(8,128)}, f32[2,2,128,128]{3,2,1,0:T(8,128)S(1)}, u32[]{:S(2)}, u32[]{:S(2)}) collective-permute-start(f32[2,2,128,128]{3,2,1,0:T(8,128)} %get-tuple-element.19), channel_id=1, source_target_pairs={{5,0},{7,2},{1,4},{3,6},{14,9},{8,11},{10,13},{12,15},{21,16},{23,... | collective-permute-start | bytes 786440 | tf_op jit(solution)/shard_map/ppermute | solution.py:251
  49.7 14.5 %collective-permute-start.6 = (f32[2,2,128,128]{3,2,1,0:T(8,128)}, f32[2,2,128,128]{3,2,1,0:T(8,128)S(1)}, u32[]{:S(2)}, u32[]{:S(2)}) collective-permute-start(f32[2,2,128,128]{3,2,1,0:T(8,128)} %get-tuple-element.18), channel_id=1, source_target_pairs={{4,0},{6,2},{0,4},{2,6},{13,9},{15,11},{9,13},{11,15},{20,16},{22,... | collective-permute-start | bytes 786440 | tf_op jit(solution)/shard_map/ppermute | solution.py:251
  64.4 1.3 copy-start.1
  65.7 1.6 %copy-start.2 = (f32[8,2,2,128,128]{4,3,2,1,0:T(8,128)S(1)}, f32[8,2,2,128,128]{4,3,2,1,0:T(8,128)}, u32[]{:S(2)}) copy-start(f32[8,2,2,128,128]{4,3,2,1,0:T(8,128)} %copy-done.1) | copy-start | bytes 6291460
  86.0 17.0 %collective-permute-start.16 = (f32[2,2,128,128]{3,2,1,0:T(8,128)}, f32[2,2,128,128]{3,2,1,0:T(8,128)S(1)}, u32[]{:S(2)}, u32[]{:S(2)}) collective-permute-start(f32[2,2,128,128]{3,2,1,0:T(8,128)} %get-tuple-element.9), channel_id=1, source_target_pairs={{0,1},{2,3},{4,5},{6,7},{9,10},{11,12},{13,14},{15,8},{16,17},{18,... | collective-permute-start | bytes 786440 | tf_op jit(solution)/shard_map/ppermute | solution.py:270
  87.7 19.4 %collective-permute-start.15 = (f32[2,2,128,128]{3,2,1,0:T(8,128)}, f32[2,2,128,128]{3,2,1,0:T(8,128)S(1)}, u32[]{:S(2)}, u32[]{:S(2)}) collective-permute-start(f32[2,2,128,128]{3,2,1,0:T(8,128)} %get-tuple-element.10), channel_id=1, source_target_pairs={{0,2},{2,4},{4,6},{6,0},{9,11},{11,13},{13,15},{15,9},{16,18},{18,... | collective-permute-start | bytes 786440 | tf_op jit(solution)/shard_map/ppermute | solution.py:270
  95.4 13.7 %collective-permute-start.14 = (f32[2,2,128,128]{3,2,1,0:T(8,128)}, f32[2,2,128,128]{3,2,1,0:T(8,128)S(1)}, u32[]{:S(2)}, u32[]{:S(2)}) collective-permute-start(f32[2,2,128,128]{3,2,1,0:T(8,128)} %get-tuple-element.11), channel_id=1, source_target_pairs={{0,3},{2,5},{4,7},{6,1},{9,12},{11,14},{13,8},{15,10},{16,19},{18,... | collective-permute-start | bytes 786440 | tf_op jit(solution)/shard_map/ppermute | solution.py:270
  96.7 19.4 %collective-permute-start.13 = (f32[2,2,128,128]{3,2,1,0:T(8,128)}, f32[2,2,128,128]{3,2,1,0:T(8,128)S(1)}, u32[]{:S(2)}, u32[]{:S(2)}) collective-permute-start(f32[2,2,128,128]{3,2,1,0:T(8,128)} %get-tuple-element.12), channel_id=1, source_target_pairs={{0,4},{2,6},{4,0},{6,2},{9,13},{11,15},{13,9},{15,11},{16,20},{18,... | collective-permute-start | bytes 786440 | tf_op jit(solution)/shard_map/ppermute | solution.py:270
  101.7 25.2 %collective-permute-start.10 = (f32[2,2,128,128]{3,2,1,0:T(8,128)}, f32[2,2,128,128]{3,2,1,0:T(8,128)S(1)}, u32[]{:S(2)}, u32[]{:S(2)}) collective-permute-start(f32[2,2,128,128]{3,2,1,0:T(8,128)} %get-tuple-element.8), channel_id=1, source_target_pairs={{0,7},{2,1},{4,3},{6,5},{9,8},{11,10},{13,12},{15,14},{16,23},{18,... | collective-permute-start | bytes 786440 | tf_op jit(solution)/shard_map/ppermute | solution.py:270
  103.0 18.2 %collective-permute-start.12 = (f32[2,2,128,128]{3,2,1,0:T(8,128)}, f32[2,2,128,128]{3,2,1,0:T(8,128)S(1)}, u32[]{:S(2)}, u32[]{:S(2)}) collective-permute-start(f32[2,2,128,128]{3,2,1,0:T(8,128)} %get-tuple-element.13), channel_id=1, source_target_pairs={{0,5},{2,7},{4,1},{6,3},{9,14},{11,8},{13,10},{15,12},{16,21},{18,... | collective-permute-start | bytes 786440 | tf_op jit(solution)/shard_map/ppermute | solution.py:270
  107.1 19.7 %collective-permute-start.11 = (f32[2,2,128,128]{3,2,1,0:T(8,128)}, f32[2,2,128,128]{3,2,1,0:T(8,128)S(1)}, u32[]{:S(2)}, u32[]{:S(2)}) collective-permute-start(f32[2,2,128,128]{3,2,1,0:T(8,128)} %get-tuple-element.14), channel_id=1, source_target_pairs={{0,6},{2,0},{4,2},{6,4},{9,15},{11,9},{13,11},{15,13},{16,22},{18,... | collective-permute-start | bytes 786440 | tf_op jit(solution)/shard_map/ppermute | solution.py:270
  127.0 17.7 %collective-permute-start.17 = (f32[4,2,2,128,128]{4,3,2,1,0:T(8,128)S(1)}, f32[4,2,2,128,128]{4,3,2,1,0:T(8,128)S(1)}, u32[]{:S(2)}, u32[]{:S(2)}) collective-permute-start(f32[4,2,2,128,128]{4,3,2,1,0:T(8,128)S(1)} %pad_maximum_fusion.own), channel_id=1, source_target_pairs={{0,8},{8,16},{16,24},{24,32},{32,40},{40,48},{48,56},{56,64},{64,7... | collective-permute-start | bytes 3145736 | tf_op jit(solution)/shard_map/ppermute | solution.py:279
  127.9 16.7 %collective-permute-start = (s32[3,4]{1,0:T(4,128)S(1)}, s32[3,4]{1,0:T(4,128)S(1)}, u32[]{:S(2)}, u32[]{:S(2)}) collective-permute-start(s32[3,4]{1,0:T(4,128)S(1)} %bitcast.80), channel_id=1, source_target_pairs={{0,8},{8,16},{16,24},{24,32},{32,40},{40,48},{48,56},{56,64},{64,7... | collective-permute-start | bytes 152 | tf_op jit(solution)/shard_map/ppermute | solution.py:280

commit v2 on v1

v2 whole, which is shorter than its diff:
```python
import functools
import math

import jax
import jax.numpy as jnp
import ml_dtypes
import numpy as np
from jax import lax
from jax.experimental import pallas as pl
from jax.experimental.pallas import tpu as pltpu
from jax.sharding import PartitionSpec as P

f32, bf16 = jnp.float32, jnp.bfloat16
phase_scale = 32.0
TILE, CUTS = "tile", "cuts"
RIGHT_A, RIGHT_A_CONJ, RIGHT_F, RIGHT_F_CONJ = range(4)


def tables(n):
    index = np.arange(n)
    dft = np.exp(-2j * np.pi * (np.outer(index, index) % n) / n) / math.sqrt(n)
    freq = np.where(index < n // 2, index, index - n).astype(np.float64)
    turn = np.exp(-1j * phase_scale * freq**2 / (n * n))
    step = np.conj(dft) @ (turn[:, None] * dft)

    def parts(matrix):
        block = np.block([[matrix.real, matrix.imag], [-matrix.imag, matrix.real]])
        high = block.astype(ml_dtypes.bfloat16)
        low = (block - high.astype(np.float64)).astype(ml_dtypes.bfloat16)
        rest = (block - high.astype(np.float64) - low.astype(np.float64)).astype(ml_dtypes.bfloat16)
        return high, low, rest

    rights, lefts = [], []
    for matrix in (step, step.conj(), dft, dft.conj()):
        high, low, rest = parts(matrix)
        rights.append(np.concatenate([high, low, rest], 0))
        lefts.append(np.concatenate([high.T, low.T, rest.T], 1))
    return np.stack(rights), np.stack(lefts)


def split(value):
    high = value.astype(bf16)
    return high, (value - high.astype(f32)).astype(bf16)


def dot(a, b):
    return jnp.dot(a, b, preferred_element_type=f32)


def right_times(re, im, table):
    n = re.shape[1]
    high, low = split(jnp.concatenate([re, im], 1))
    parts = jnp.concatenate([table[: 2 * n], table[...]], 0)
    out = dot(jnp.concatenate([low, high, high, high], 1), parts)
    return out[:, :n], out[:, n:]


def left_times(re, im, table):
    n = re.shape[0]
    high, low = split(jnp.concatenate([re, im], 0))
    main = dot(table[:, : 2 * n], jnp.concatenate([high, low], 1))
    rest = dot(table[:, 2 * n :], jnp.concatenate([high, high], 0))
    out = main[:, :n] + main[:, n:] + rest
    return out[:n], out[n:]


def both_sides(re, im, rights, lefts, which):
    re, im = right_times(re, im, rights.at[which])
    return left_times(re, im, lefts.at[which])


def fused_kernel(
    places,
    places_before,
    probe,
    counts,
    real_hbm,
    imag_hbm,
    rights_hbm,
    lefts_hbm,
    own_out,
    other_out,
    real,
    imag,
    rights,
    lefts,
    rim_out,
    rim_in,
    merged,
    patches,
    psi,
    contrib,
    load_sem,
    table_sem,
    rim_send,
    rim_recv,
    gather_send,
    gather_recv,
    back_send,
    back_recv,
    ahead_send,
    ahead_recv,
):
    cuts, tiles = lax.axis_size(CUTS), lax.axis_size(TILE)
    me, tile = lax.axis_index(CUTS), lax.axis_index(TILE)
    above = lax.rem(tile + tiles - 1, tiles)
    below = lax.rem(tile + 1, tiles)
    slices, rows, cols = real.shape
    n = probe.shape[1]
    count = merged.shape[0]
    total = cuts * slices
    spread = cuts // count
    phase = lax.rem(tile, spread)
    mine = lax.div(lax.rem(me - phase + cuts, cuts), spread)

    def device(t, z):
        return dict(device_id=(t, z), device_id_type=pl.DeviceIdType.MESH)

    loads = []
    for i, (source, target) in enumerate(((real_hbm, real), (imag_hbm, imag))):
        for s in range(slices):
            loads.append(pltpu.make_async_copy(source.at[s], target.at[s], load_sem.at[i, s]))
    table_loads = [
        pltpu.make_async_copy(rights_hbm, rights, table_sem.at[0]),
        pltpu.make_async_copy(lefts_hbm, lefts, table_sem.at[1]),
    ]
    for copy in loads + table_loads:
        copy.start()

    barrier = pltpu.get_barrier_semaphore()
    for d in range(1, cuts):
        pl.semaphore_signal(barrier, inc=1, **device(tile, lax.rem(me + d, cuts)))
    pl.semaphore_signal(barrier, inc=1, **device(above, me))
    pl.semaphore_signal(barrier, inc=1, **device(below, me))

    row_at = lax.broadcasted_iota(jnp.int32, (n, n), 0)
    col_at = lax.broadcasted_iota(jnp.int32, (n, n), 1)

    def window(where, k, target, own):
        row = lax.rem(where[k, 0], n)
        column = where[k, 1]
        block = lax.div(column, n)
        keep = row_at >= row if own else row_at < row
        wanted = jnp.where(col_at >= column - block * n, block, block + 1)
        for s in range(slices):
            for i, source in enumerate((real, imag)):
                value = jnp.zeros((n, n), f32)
                for at in range(cols // n):
                    value = jnp.where(wanted == at, source[s, :, at * n : (at + 1) * n], value)
                target[k, s, i] = jnp.where(keep, value, 0.0)

    def turn(j):
        return lax.rem(lax.div(me, spread) + j, count)

    def rim_copy(k):
        return pltpu.make_async_remote_copy(
            rim_out.at[k], rim_in.at[k], rim_send.at[k], rim_recv.at[k], **device(above, me)
        )

    def owner(k):
        return lax.rem(k * spread + phase, cuts)

    def gather_copy(k):
        return pltpu.make_async_remote_copy(
            merged.at[k], patches.at[me], gather_send.at[k], gather_recv.at[me], **device(tile, owner(k))
        )

    def arrival(z):
        return pltpu.make_async_remote_copy(
            merged.at[0], patches.at[z], gather_send.at[0], gather_recv.at[z], **device(tile, z)
        )

    for copy in loads:
        copy.wait()
    pl.semaphore_wait(barrier, cuts + 1)

    def send_rim(j, carry):
        k = turn(j)
        window(places_before, k, rim_out, False)
        rim_copy(k).start()
        return carry

    lax.fori_loop(0, count, send_rim, 0)

    def take_own(j, carry):
        window(places, turn(j), merged, True)
        return carry

    lax.fori_loop(0, count, take_own, 0)

    def send_windows(j, carry):
        k = turn(j)
        rim_copy(k).wait_recv()
        for s in range(slices):
            for i in range(2):
                merged[k, s, i] = merged[k, s, i] + rim_in[k, s, i]

        @pl.when(owner(k) != me)
        def _():
            gather_copy(k).start()

        @pl.when(owner(k) == me)
        def _():
            for s in range(slices):
                for i in range(2):
                    patches[me, s, i] = merged[k, s, i]

        return carry

    lax.fori_loop(0, count, send_windows, 0)
    for copy in table_loads:
        copy.wait()

    def back_copy(s):
        inner = lax.rem(s, slices)
        return pltpu.make_async_remote_copy(
            contrib.at[s],
            own_out.at[mine, inner],
            back_send.at[s],
            back_recv.at[mine, inner],
            **device(tile, lax.div(s, slices)),
        )

    def keep_copy(s):
        return pltpu.make_async_copy(
            contrib.at[s], own_out.at[mine, lax.rem(s, slices)], back_send.at[s]
        )

    def put(s, re, im):
        a, b = psi[s, 0], psi[s, 1]
        contrib[s, 0] = a * re + b * im
        contrib[s, 1] = a * im - b * re
        z = lax.div(s, slices)

        @pl.when(z != me)
        def _():
            back_copy(s).start()

        @pl.when(z == me)
        def _():
            keep_copy(s).start()

    def patch_at(s):
        z, inner = lax.div(s, slices), lax.rem(s, slices)
        return patches[z, inner, 0], patches[z, inner, 1]

    @pl.when(owner(mine) == me)
    def _():
        row, column = lax.rem(places[mine, 0], n), lax.rem(places[mine, 1], n)
        a, b = probe[0], probe[1]
        bit = 1
        while bit < n:
            for axis, amount in ((0, row), (1, column)):
                take = (jnp.full((n, n), amount, jnp.int32) & bit) > 0
                a = jnp.where(take, pltpu.roll(a, bit, axis), a)
                b = jnp.where(take, pltpu.roll(b, bit, axis), b)
            bit *= 2
        psi[0, 0] = a
        psi[0, 1] = b

        def forward(s, carry):
            z = lax.div(s, slices)

            @pl.when((lax.rem(s, slices) == 0) & (z != me))
            def _():
                arrival(z).wait_recv()

            a, b = psi[s, 0], psi[s, 1]
            p, q = patch_at(s)
            re, im = both_sides(p * a - q * b, p * b + q * a, rights, lefts, RIGHT_A)
            psi[s + 1, 0] = re
            psi[s + 1, 1] = im
            return carry

        lax.fori_loop(0, total - 1, forward, 0)
        a, b = psi[total - 1, 0], psi[total - 1, 1]
        p, q = patch_at(total - 1)
        re, im = both_sides(p * a - q * b, p * b + q * a, rights, lefts, RIGHT_F)
        weight = 4.0 * (re * re + im * im - counts[mine].astype(f32))
        re, im = both_sides(weight * re, weight * im, rights, lefts, RIGHT_F_CONJ)
        put(total - 1, re, im)

        def backward(i, carry):
            re, im = carry
            s = total - 1 - i
            p, q = patch_at(s)
            re, im = both_sides(p * re + q * im, p * im - q * re, rights, lefts, RIGHT_A_CONJ)
            put(s - 1, re, im)
            return re, im

        lax.fori_loop(0, total - 1, backward, (re, im))

    def term_copy(k, s):
        return pltpu.make_async_remote_copy(
            contrib.at[0], own_out.at[k, s], back_send.at[0], back_recv.at[k, s], **device(tile, owner(k))
        )

    def ahead_copy(k, s):
        return pltpu.make_async_remote_copy(
            own_out.at[k, s], other_out.at[k, s], ahead_send.at[k, s], ahead_recv.at[k, s], **device(below, me)
        )

    def pass_on(step, carry):
        s = slices - 1 - lax.div(step, count)
        k = turn(lax.rem(step, count))

        @pl.when(owner(k) != me)
        def _():
            term_copy(k, s).wait_recv()

        @pl.when(owner(k) == me)
        def _():
            keep_copy(me * slices + s).wait()

        ahead_copy(k, s).start()
        return carry

    lax.fori_loop(0, count * slices, pass_on, 0)

    def finish(step, carry):
        s, k = lax.div(step, count), lax.rem(step, count)
        ahead_copy(k, s).wait()
        return carry

    lax.fori_loop(0, count * slices, finish, 0)

    def finish_windows(k, carry):
        rim_copy(k).wait_send()

        @pl.when(owner(k) != me)
        def _():
            gather_copy(k).wait_send()

        return carry

    lax.fori_loop(0, count, finish_windows, 0)

    @pl.when(owner(mine) == me)
    def _():
        def finish_back(s, carry):
            @pl.when(lax.div(s, slices) != me)
            def _():
                back_copy(s).wait_send()

            return carry

        lax.fori_loop(0, total, finish_back, 0)


def add_kernel(places, places_before, own, other, real, imag):
    n = own.shape[-1]
    count = own.shape[0]
    rows = lax.broadcasted_iota(jnp.int32, (n, n), 0)
    cols = lax.broadcasted_iota(jnp.int32, (n, n), 1)
    last = real.shape[2] // n - 1
    real[...] = jnp.zeros_like(real)
    imag[...] = jnp.zeros_like(imag)
    for where, source, is_own in ((places, own, True), (places_before, other, False)):
        for k in range(count):
            row = lax.rem(where[k, 0], n)
            column = where[k, 1]
            block = lax.div(column, n)
            keep = (rows >= row) if is_own else (rows < row)
            here = pl.ds(pl.multiple_of(block * n, n), n)
            beside = pl.ds(pl.multiple_of(jnp.minimum(block + 1, last) * n, n), n)
            first = cols >= column - block * n
            for i, target in enumerate((real, imag)):
                value = jnp.where(keep, source[k, 0, i], 0.0)
                target[0, :, here] += jnp.where(first, value, 0.0)
                target[0, :, beside] += jnp.where(first, 0.0, value)


def add(places, places_before, own, other, shape):
    slices, rows, cols = shape
    count, _, _, n, _ = own.shape
    window = pl.BlockSpec((count, 1, 2, n, n), lambda s, *_: (0, s, 0, 0, 0))
    strip = pl.BlockSpec((1, rows, cols), lambda s, *_: (s, 0, 0))
    return pl.pallas_call(
        add_kernel,
        out_shape=(jax.ShapeDtypeStruct(shape, f32),) * 2,
        grid_spec=pltpu.PrefetchScalarGridSpec(
            num_scalar_prefetch=2,
            grid=(slices,),
            in_specs=[window, window],
            out_specs=(strip, strip),
        ),
        compiler_params=pltpu.CompilerParams(vmem_limit_bytes=32 << 20),
    )(places, places_before, own, other)


def shards(object_real, object_imag, probe, positions, counts):
    cuts, tiles = lax.axis_size(CUTS), lax.axis_size(TILE)
    slices, rows, cols = object_real.shape
    n = probe.shape[1]
    count = positions.shape[0]
    before = lax.ppermute(positions, TILE, [(t, (t + 1) % tiles) for t in range(tiles)])
    rights, lefts = (jnp.asarray(t) for t in tables(n))
    windows = (count, slices, 2, n, n)
    total = cuts * slices
    vmem = pl.BlockSpec(memory_space=pltpu.VMEM)
    smem = pl.BlockSpec(memory_space=pltpu.SMEM)
    hbm = pl.BlockSpec(memory_space=pl.ANY)
    dma = pltpu.SemaphoreType.DMA
    own, other = pl.pallas_call(
        fused_kernel,
        out_shape=(jax.ShapeDtypeStruct(windows, f32),) * 2,
        in_specs=[smem, smem, vmem, vmem, hbm, hbm, hbm, hbm],
        out_specs=(hbm, hbm),
        scratch_shapes=[
            pltpu.VMEM(object_real.shape, f32),
            pltpu.VMEM(object_imag.shape, f32),
            pltpu.VMEM(rights.shape, bf16),
            pltpu.VMEM(lefts.shape, bf16),
            pltpu.VMEM(windows, f32),
            pltpu.VMEM(windows, f32),
            pltpu.VMEM(windows, f32),
            pltpu.VMEM((cuts, slices, 2, n, n), f32),
            pltpu.VMEM((total, 2, n, n), f32),
            pltpu.VMEM((total, 2, n, n), f32),
            dma((2, slices)),
            dma((2,)),
            dma((count,)),
            dma((count,)),
            dma((count,)),
            dma((cuts,)),
            dma((total,)),
            dma((count, slices)),
            dma((count, slices)),
            dma((count, slices)),
        ],
        compiler_params=pltpu.CompilerParams(
            collective_id=0, has_side_effects=True, vmem_limit_bytes=40 << 20
        ),
    )(positions, before, probe, counts, object_real, object_imag, rights, lefts)
    return add(positions, before, own, other, object_real.shape)


def solution(mesh):
    placed = (
        P("cuts", "tile", None),
        P("cuts", "tile", None),
        P(),
        P("tile", None),
        P("tile", None, None),
    )
    return jax.shard_map(
        shards,
        mesh=mesh,
        in_specs=placed,
        out_specs=(P("cuts", "tile", None), P("cuts", "tile", None)),
        check_vma=False,
    )
```

time: 149 us -> 105 us (0.70)
  the two profiles are of different devices: /device:TPU:0 before, /device:TPU:1 now
where the time goes in v2:
time: 105 us
  Pallas kernels  91.6 us (87%)
  local copies, waits for them, and re-layouts  8.62 us (8%)
  starting transfers between devices  2.69 us (3%)
  waiting for transfers between devices  1.2 us (1%)
    pallas_call x1, Pallas kernels, shards(): pl.pallas_call(fused_kernel, out_shape=(jax.ShapeDtypeStruct(windows, f32...  88.3 us
    unnamed x13, local copies, waits for them, and re-layouts  8.62 us
    pallas_call x1, Pallas kernels, add(): pl.pallas_call(add_kernel, out_shape=(jax.ShapeDtypeStruct(shape, f32),)...  3.29 us
    ppermute x1, starting transfers between devices, shards(): lax.ppermute(positions, TILE, [(t, (t + 1) % tiles) for t in range(tiles)])  2.69 us
  transfers between devices with their start and end apart: 1, of which 1 were waited for; matrix products, arithmetic and copies ran while one was open for 0% of the time, Pallas kernels for 0%

profile of v2, /device:TPU:1, one launch (start us, length us, event | category | flops | bytes accessed | tf_op | source)
XLA Modules:
  0.0 104.7 jit_solution(13684316543712268336)
XLA Ops:
  0.6 0.8 copy.11.places
  1.4 2.7 %collective-permute-start = (s32[4,2]{1,0:T(4,128)S(1)}, s32[4,2]{1,0:T(4,128)S(1)}, u32[]{:S(2)}, u32[]{:S(2)}) collective-permute-start(s32[4,2]{1,0:T(4,128)S(1)} %copy.11.places), channel_id=1, source_target_pairs={{0,8},{8,16},{16,24},{24,32},{32,40},{40,48},{48,56},{56,64},{64,7... | collective-permute-start | bytes 104 | tf_op jit(solution)/shard_map/ppermute | solution.py:396
  4.1 1.2 %collective-permute-done.places_before = s32[4,2]{1,0:T(4,128)S(1)} collective-permute-done((s32[4,2]{1,0:T(4,128)S(1)}, s32[4,2]{1,0:T(4,128)S(1)}, u32[]{:S(2)}, u32[]{:S(2)}) %collective-permute-start) | collective-permute-done | bytes 64 | tf_op jit(solution)/shard_map/ppermute | solution.py:396
  5.3 0.0 copy-start
  5.3 1.6 %copy-done = f32[2,128,2048]{2,1,0:T(8,128)S(1)} copy-done((f32[2,128,2048]{2,1,0:T(8,128)S(1)}, f32[2,128,2048]{2,1,0:T(8,128)}, u32[]{:S(2)}) %copy-start) | copy-done | bytes 2097176
  6.9 0.0 copy-start.1
  6.9 1.6 %copy-done.1 = f32[2,128,2048]{2,1,0:T(8,128)S(1)} copy-done((f32[2,128,2048]{2,1,0:T(8,128)S(1)}, f32[2,128,2048]{2,1,0:T(8,128)}, u32[]{:S(2)}) %copy-start.1) | copy-done | bytes 2097176
  8.5 0.0 copy-start.2
  8.5 1.4 %copy-done.2 = bf16[4,256,768]{2,1,0:T(8,128)(2,1)S(1)} copy-done((bf16[4,256,768]{2,1,0:T(8,128)(2,1)S(1)}, bf16[4,256,768]{2,1,0:T(8,128)(2,1)}, u32[]{:S(2)}) %copy-start.2) | copy-done | bytes 1572888
  9.9 0.0 copy-start.3
  9.9 1.4 %copy-done.3 = bf16[4,768,256]{2,1,0:T(8,128)(2,1)S(1)} copy-done((bf16[4,768,256]{2,1,0:T(8,128)(2,1)S(1)}, bf16[4,768,256]{2,1,0:T(8,128)(2,1)}, u32[]{:S(2)}) %copy-start.3) | copy-done | bytes 1572888
  11.3 0.0 copy-start.4
  11.3 0.9 copy-done.4
  12.2 0.0 copy-start.5
  12.2 0.9 copy-done.5
  13.1 88.3 %shard_map.86 = (f32[4,2,2,128,128]{4,3,2,1,0:T(8,128)S(1)}, f32[4,2,2,128,128]{4,3,2,1,0:T(8,128)S(1)}) custom-call(s32[4,2]{1,0:T(4,128)S(1)} %copy.11.places, s32[4,2]{1,0:T(4,128)S(1)} %collective-permute-done.places_before, f32[2,128,128]{2,1,0:T(8,128)S(1)} %copy-done.5, s32[4,128,128]{2,1,0:T(8,128)S(1)} %copy-done.4, f32[2,128,2048]{2,1,0:T(8,128)S(1)} %copy-done, ...), custom_call_target="tpu_custom_call" | custom-call | tf_op jit(solution)/shard_map/pallas_call | solution.py:404
  101.5 3.3 %shard_map.87 = (f32[2,128,2048]{2,1,0:T(8,128)}, f32[2,128,2048]{2,1,0:T(8,128)}) custom-call(s32[4,2]{1,0:T(4,128)S(1)} %copy.11.places, s32[4,2]{1,0:T(4,128)S(1)} %collective-permute-done.places_before, f32[4,2,2,128,128]{4,3,2,1,0:T(8,128)S(1)} %get-tuple-element.4.own, f32[4,2,2,128,128]{4,3,2,1,0:T(8,128)S(1)} %get-tuple-element.5.other), custom_call_target="tpu_custom_call" | custom-call | tf_op jit(solution)/shard_map/pallas_call | solution.py:378
Async XLA Ops:
  1.4 3.9 %collective-permute-start = (s32[4,2]{1,0:T(4,128)S(1)}, s32[4,2]{1,0:T(4,128)S(1)}, u32[]{:S(2)}, u32[]{:S(2)}) collective-permute-start(s32[4,2]{1,0:T(4,128)S(1)} %copy.11.places), channel_id=1, source_target_pairs={{0,8},{8,16},{16,24},{24,32},{32,40},{40,48},{48,56},{56,64},{64,7... | collective-permute-start | bytes 104 | tf_op jit(solution)/shard_map/ppermute | solution.py:396
  5.3 1.6 %copy-start = (f32[2,128,2048]{2,1,0:T(8,128)S(1)}, f32[2,128,2048]{2,1,0:T(8,128)}, u32[]{:S(2)}) copy-start(f32[2,128,2048]{2,1,0:T(8,128)} %real_hbm.1) | copy-start | bytes 6291460
  6.9 1.6 %copy-start.1 = (f32[2,128,2048]{2,1,0:T(8,128)S(1)}, f32[2,128,2048]{2,1,0:T(8,128)}, u32[]{:S(2)}) copy-start(f32[2,128,2048]{2,1,0:T(8,128)} %imag_hbm.1) | copy-start | bytes 6291460
  8.5 1.4 %copy-start.2 = (bf16[4,256,768]{2,1,0:T(8,128)(2,1)S(1)}, bf16[4,256,768]{2,1,0:T(8,128)(2,1)}, u32[]{:S(2)}) copy-start(bf16[4,256,768]{2,1,0:T(8,128)(2,1)} %constant.5.clone.lefts_hbm) | copy-start | bytes 4718596
  9.9 1.4 %copy-start.3 = (bf16[4,768,256]{2,1,0:T(8,128)(2,1)S(1)}, bf16[4,768,256]{2,1,0:T(8,128)(2,1)}, u32[]{:S(2)}) copy-start(bf16[4,768,256]{2,1,0:T(8,128)(2,1)} %constant.4.clone.rights_hbm) | copy-start | bytes 4718596
  11.3 0.9 copy-start.4
  12.2 0.9 copy-start.5

commit v3 on v2

--- a/solution.py
+++ b/solution.py
@@ -3,7 +3,6 @@
 
 import jax
 import jax.numpy as jnp
-import ml_dtypes
 import numpy as np
 from jax import lax
 from jax.experimental import pallas as pl
@@ -23,19 +22,11 @@
     turn = np.exp(-1j * phase_scale * freq**2 / (n * n))
     step = np.conj(dft) @ (turn[:, None] * dft)
 
-    def parts(matrix):
+    out = []
+    for matrix in (step, dft):
         block = np.block([[matrix.real, matrix.imag], [-matrix.imag, matrix.real]])
-        high = block.astype(ml_dtypes.bfloat16)
-        low = (block - high.astype(np.float64)).astype(ml_dtypes.bfloat16)
-        rest = (block - high.astype(np.float64) - low.astype(np.float64)).astype(ml_dtypes.bfloat16)
-        return high, low, rest
-
-    rights, lefts = [], []
-    for matrix in (step, step.conj(), dft, dft.conj()):
-        high, low, rest = parts(matrix)
-        rights.append(np.concatenate([high, low, rest], 0))
-        lefts.append(np.concatenate([high.T, low.T, rest.T], 1))
-    return np.stack(rights), np.stack(lefts)
+        out += [block, block.T]
+    return np.stack(out).astype(np.float32)
 
 
 def split(value):
@@ -72,16 +63,18 @@
 def fused_kernel(
     places,
     places_before,
-    probe,
-    counts,
+    probe_hbm,
+    counts_hbm,
     real_hbm,
     imag_hbm,
-    rights_hbm,
-    lefts_hbm,
+    blocks_hbm,
     own_out,
     other_out,
     real,
     imag,
+    probe,
+    counts,
+    blocks,
     rights,
     lefts,
     rim_out,
@@ -92,6 +85,8 @@
     contrib,
     load_sem,
     table_sem,
+    counts_send,
+    counts_recv,
     rim_send,
     rim_recv,
     gather_send,
@@ -112,6 +107,8 @@
     spread = cuts // count
     phase = lax.rem(tile, spread)
     mine = lax.div(lax.rem(me - phase + cuts, cuts), spread)
+    is_owner = lax.rem(me - phase + cuts, spread) == 0
+    half = count // 2
 
     def device(t, z):
         return dict(device_id=(t, z), device_id_type=pl.DeviceIdType.MESH)
@@ -121,9 +118,20 @@
         for s in range(slices):
             loads.append(pltpu.make_async_copy(source.at[s], target.at[s], load_sem.at[i, s]))
     table_loads = [
-        pltpu.make_async_copy(rights_hbm, rights, table_sem.at[0]),
-        pltpu.make_async_copy(lefts_hbm, lefts, table_sem.at[1]),
+        pltpu.make_async_copy(blocks_hbm, blocks, table_sem.at[0]),
+        pltpu.make_async_copy(probe_hbm, probe, table_sem.at[1]),
     ]
+    own_counts = pltpu.make_async_copy(counts_hbm.at[mine], counts, counts_recv.at[0])
+    below_slot = lax.rem(me - lax.rem(below, spread) + cuts, cuts)
+    below_owns = (lax.rem(below_slot, spread) == 0) & (lax.div(below_slot, spread) >= half)
+    next_counts = pltpu.make_async_remote_copy(
+        counts_hbm.at[lax.div(below_slot, spread)],
+        counts,
+        counts_send.at[0],
+        counts_recv.at[0],
+        **device(below, me),
+    )
+
     for copy in loads + table_loads:
         copy.start()
 
@@ -136,11 +144,12 @@
     row_at = lax.broadcasted_iota(jnp.int32, (n, n), 0)
     col_at = lax.broadcasted_iota(jnp.int32, (n, n), 1)
 
-    def window(where, k, target, own):
-        row = lax.rem(where[k, 0], n)
-        column = where[k, 1]
+    def window(k, target, own):
+        row = lax.rem(jnp.where(own, places[0, k], places_before[0, k]), n)
+        column = jnp.where(own, places[1, k], places_before[1, k])
         block = lax.div(column, n)
-        keep = row_at >= row if own else row_at < row
+        lower = (row_at >= row).astype(jnp.int32)
+        keep = lower == own.astype(jnp.int32)
         wanted = jnp.where(col_at >= column - block * n, block, block + 1)
         for s in range(slices):
             for i, source in enumerate((real, imag)):
@@ -149,12 +158,13 @@
                     value = jnp.where(wanted == at, source[s, :, at * n : (at + 1) * n], value)
                 target[k, s, i] = jnp.where(keep, value, 0.0)
 
-    def turn(j):
-        return lax.rem(lax.div(me, spread) + j, count)
+    def turn(j, near):
+        group = lax.rem(lax.div(j, half) + lax.rem(tile, 2) + (0 if near else 1), 2)
+        return group * half + lax.rem(lax.div(me, spread) + j, half)
 
     def rim_copy(k):
         return pltpu.make_async_remote_copy(
-            rim_out.at[k], rim_in.at[k], rim_send.at[k], rim_recv.at[k], **device(above, me)
+            rim_out.at[k], rim_in.at[k], rim_send.at[k], rim_recv.at[k], **device(jnp.where(k < half, above, below), me)
         )
 
     def owner(k):
@@ -175,21 +185,31 @@
     pl.semaphore_wait(barrier, cuts + 1)
 
     def send_rim(j, carry):
-        k = turn(j)
-        window(places_before, k, rim_out, False)
+        k = turn(j, False)
+        window(k, rim_out, k >= half)
         rim_copy(k).start()
         return carry
 
     lax.fori_loop(0, count, send_rim, 0)
 
+    @pl.when(below_owns)
+    def _():
+        next_counts.start()
+
+    @pl.when(is_owner & (mine < half))
+    def _():
+        own_counts.start()
+
+
     def take_own(j, carry):
-        window(places, turn(j), merged, True)
+        k = turn(j, True)
+        window(k, merged, k < half)
         return carry
 
     lax.fori_loop(0, count, take_own, 0)
 
     def send_windows(j, carry):
-        k = turn(j)
+        k = turn(j, True)
         rim_copy(k).wait_recv()
         for s in range(slices):
             for i in range(2):
@@ -207,9 +227,21 @@
 
         return carry
 
-    lax.fori_loop(0, count, send_windows, 0)
     for copy in table_loads:
         copy.wait()
+
+    @pl.when(is_owner)
+    def _():
+        for i in range(blocks.shape[0]):
+            which, other = (i // 2) * 2 + i % 2, (i // 2) * 2 + 1 - i % 2
+            high = blocks[i].astype(bf16)
+            low, rest = split(blocks[i] - high.astype(f32))
+            for j, part in enumerate((high, low, rest)):
+                at = slice(j * 2 * n, (j + 1) * 2 * n)
+                rights[which, at, :] = part
+                lefts[other, :, at] = part
+
+    lax.fori_loop(0, count, send_windows, 0)
 
     def back_copy(s):
         inner = lax.rem(s, slices)
@@ -244,9 +276,10 @@
         z, inner = lax.div(s, slices), lax.rem(s, slices)
         return patches[z, inner, 0], patches[z, inner, 1]
 
-    @pl.when(owner(mine) == me)
+    @pl.when(is_owner)
     def _():
-        row, column = lax.rem(places[mine, 0], n), lax.rem(places[mine, 1], n)
+        row = lax.rem(jnp.where(mine < half, places[0, mine], places_before[0, mine]), n)
+        column = lax.rem(jnp.where(mine < half, places[1, mine], places_before[1, mine]), n)
         a, b = probe[0], probe[1]
         bit = 1
         while bit < n:
@@ -276,7 +309,16 @@
         a, b = psi[total - 1, 0], psi[total - 1, 1]
         p, q = patch_at(total - 1)
         re, im = both_sides(p * a - q * b, p * b + q * a, rights, lefts, RIGHT_F)
-        weight = 4.0 * (re * re + im * im - counts[mine].astype(f32))
+
+        @pl.when(mine < half)
+        def _():
+            own_counts.wait()
+
+        @pl.when(mine >= half)
+        def _():
+            next_counts.wait_recv()
+
+        weight = 4.0 * (re * re + im * im - counts[...].astype(f32))
         re, im = both_sides(weight * re, weight * im, rights, lefts, RIGHT_F_CONJ)
         put(total - 1, re, im)
 
@@ -297,12 +339,12 @@
 
     def ahead_copy(k, s):
         return pltpu.make_async_remote_copy(
-            own_out.at[k, s], other_out.at[k, s], ahead_send.at[k, s], ahead_recv.at[k, s], **device(below, me)
+            own_out.at[k, s], other_out.at[k, s], ahead_send.at[k, s], ahead_recv.at[k, s], **device(jnp.where(k < half, below, above), me)
         )
 
     def pass_on(step, carry):
-        s = slices - 1 - lax.div(step, count)
-        k = turn(lax.rem(step, count))
+        s = slices - 1 - lax.rem(lax.div(step, half), slices)
+        k = turn(lax.div(step, half * slices) * half + lax.rem(step, half), False)
 
         @pl.when(owner(k) != me)
         def _():
@@ -335,7 +377,12 @@
 
     lax.fori_loop(0, count, finish_windows, 0)
 
-    @pl.when(owner(mine) == me)
+    @pl.when(below_owns)
+    def _():
+        next_counts.wait_send()
+
+
+    @pl.when(is_owner)
     def _():
         def finish_back(s, carry):
             @pl.when(lax.div(s, slices) != me)
@@ -355,10 +402,12 @@
     last = real.shape[2] // n - 1
     real[...] = jnp.zeros_like(real)
     imag[...] = jnp.zeros_like(imag)
-    for where, source, is_own in ((places, own, True), (places_before, other, False)):
+    for source, first_own in ((own, True), (other, False)):
         for k in range(count):
-            row = lax.rem(where[k, 0], n)
-            column = where[k, 1]
+            is_own = (k < count // 2) == first_own
+            where = places if is_own else places_before
+            row = lax.rem(where[0, k], n)
+            column = where[1, k]
             block = lax.div(column, n)
             keep = (rows >= row) if is_own else (rows < row)
             here = pl.ds(pl.multiple_of(block * n, n), n)
@@ -384,7 +433,7 @@
             in_specs=[window, window],
             out_specs=(strip, strip),
         ),
-        compiler_params=pltpu.CompilerParams(vmem_limit_bytes=32 << 20),
+        compiler_params=pltpu.CompilerParams(vmem_limit_bytes=62 << 20),
     )(places, places_before, own, other)
 
 
@@ -393,24 +442,27 @@
     slices, rows, cols = object_real.shape
     n = probe.shape[1]
     count = positions.shape[0]
+    positions = positions.T
     before = lax.ppermute(positions, TILE, [(t, (t + 1) % tiles) for t in range(tiles)])
-    rights, lefts = (jnp.asarray(t) for t in tables(n))
+    blocks = jnp.asarray(tables(n))
     windows = (count, slices, 2, n, n)
     total = cuts * slices
-    vmem = pl.BlockSpec(memory_space=pltpu.VMEM)
     smem = pl.BlockSpec(memory_space=pltpu.SMEM)
-    hbm = pl.BlockSpec(memory_space=pl.ANY)
+    hbm = pl.BlockSpec(memory_space=pltpu.HBM)
     dma = pltpu.SemaphoreType.DMA
     own, other = pl.pallas_call(
         fused_kernel,
         out_shape=(jax.ShapeDtypeStruct(windows, f32),) * 2,
-        in_specs=[smem, smem, vmem, vmem, hbm, hbm, hbm, hbm],
+        in_specs=[smem, smem, hbm, hbm, hbm, hbm, hbm],
         out_specs=(hbm, hbm),
         scratch_shapes=[
             pltpu.VMEM(object_real.shape, f32),
             pltpu.VMEM(object_imag.shape, f32),
-            pltpu.VMEM(rights.shape, bf16),
-            pltpu.VMEM(lefts.shape, bf16),
+            pltpu.VMEM(probe.shape, f32),
+            pltpu.VMEM((n, n), jnp.int32),
+            pltpu.VMEM(blocks.shape, f32),
+            pltpu.VMEM((4, 6 * n, 2 * n), bf16),
+            pltpu.VMEM((4, 2 * n, 6 * n), bf16),
             pltpu.VMEM(windows, f32),
             pltpu.VMEM(windows, f32),
             pltpu.VMEM(windows, f32),
@@ -419,6 +471,8 @@
             pltpu.VMEM((total, 2, n, n), f32),
             dma((2, slices)),
             dma((2,)),
+            dma((1,)),
+            dma((1,)),
             dma((count,)),
             dma((count,)),
             dma((count,)),
@@ -429,9 +483,9 @@
             dma((count, slices)),
         ],
         compiler_params=pltpu.CompilerParams(
-            collective_id=0, has_side_effects=True, vmem_limit_bytes=40 << 20
+            collective_id=0, has_side_effects=True, vmem_limit_bytes=62 << 20
         ),
-    )(positions, before, probe, counts, object_real, object_imag, rights, lefts)
+    )(positions, before, probe, counts, object_real, object_imag, blocks)
     return add(positions, before, own, other, object_real.shape)
 
 

time: 105 us -> 88.9 us (0.85)
  Pallas kernels: 91.6 us -> 82.8 us
  local copies, waits for them, and re-layouts: 8.62 us -> 0.52 us
    pallas_call x1, Pallas kernels: 88.3 us -> 78.3 us  [shards(): pl.pallas_call(fused_kernel, out_shape=(jax.ShapeDtypeStruct(windows, f32...]
    unnamed x13 -> x2, local copies, waits for them, and re-layouts: 8.62 us -> 0.52 us
    pallas_call x1, Pallas kernels: 3.29 us -> 4.45 us  [add(): pl.pallas_call(add_kernel, out_shape=(jax.ShapeDtypeStruct(shape, f32),)...]
where the time goes in v3:
time: 88.9 us; the launch traced here: 88.1 us
  Pallas kernels  82.8 us (93%)
  starting transfers between devices  2.76 us (3%)
  waiting for transfers between devices  1.4 us (2%)
    pallas_call x1, Pallas kernels, shards(): pl.pallas_call(fused_kernel, out_shape=(jax.ShapeDtypeStruct(windows, f32...  78.3 us
    pallas_call x1, Pallas kernels, add(): pl.pallas_call(add_kernel, out_shape=(jax.ShapeDtypeStruct(shape, f32),)...  4.45 us
    ppermute x1, starting transfers between devices, shards(): lax.ppermute(positions, TILE, [(t, (t + 1) % tiles) for t in range(tiles)])  2.76 us
  transfers between devices with their start and end apart: 1, of which 1 were waited for; matrix products, arithmetic and copies ran while one was open for 0% of the time, Pallas kernels for 0%

profile of v3, /device:TPU:1, one launch (start us, length us, event | category | flops | bytes accessed | tf_op | source)
XLA Modules:
  0.0 88.1 jit_solution(12286429614738782252)
XLA Ops:
  0.6 2.8 %collective-permute-start = (s32[2,4]{1,0:T(2,128)}, s32[2,4]{1,0:T(2,128)S(1)}, u32[]{:S(2)}, u32[]{:S(2)}) collective-permute-start(s32[2,4]{1,0:T(2,128)} %bitcast.1), channel_id=1, source_target_pairs={{0,8},{8,16},{16,24},{24,32},{32,40},{40,48},{48,56},{56,64},{64,7... | collective-permute-start | bytes 104 | tf_op jit(solution)/shard_map/ppermute | solution.py:446
  3.4 1.4 %collective-permute-done.places_before = s32[2,4]{1,0:T(2,128)S(1)} collective-permute-done((s32[2,4]{1,0:T(2,128)}, s32[2,4]{1,0:T(2,128)S(1)}, u32[]{:S(2)}, u32[]{:S(2)}) %collective-permute-start) | collective-permute-done | bytes 64 | tf_op jit(solution)/shard_map/ppermute | solution.py:446
  4.8 0.0 copy-start
  4.8 0.5 copy-done
  5.3 78.3 %shard_map.77 = (f32[4,2,2,128,128]{4,3,2,1,0:T(8,128)}, f32[4,2,2,128,128]{4,3,2,1,0:T(8,128)}) custom-call(s32[2,4]{1,0:T(2,128)} %bitcast.2, s32[2,4]{1,0:T(2,128)} %copy-done, f32[2,128,128]{2,1,0:T(8,128)} %probe_hbm.1, s32[4,128,128]{2,1,0:T(8,128)} %counts_hbm.1, f32[2,128,2048]{2,1,0:T(8,128)} %real_hbm.1, f32[2,128,2048]{2,1,0:T(8,128)} %imag_hbm.1, ...), custom_call_target="tpu_custom_call" | custom-call | tf_op jit(solution)/shard_map/pallas_call | solution.py:453
  83.7 4.4 %shard_map.78 = (f32[2,128,2048]{2,1,0:T(8,128)}, f32[2,128,2048]{2,1,0:T(8,128)}) custom-call(s32[2,4]{1,0:T(2,128)} %bitcast.3, s32[2,4]{1,0:T(2,128)} %copy-done, f32[4,2,2,128,128]{4,3,2,1,0:T(8,128)} %get-tuple-element.4.own, f32[4,2,2,128,128]{4,3,2,1,0:T(8,128)} %get-tuple-element.5.other), custom_call_target="tpu_custom_call" | custom-call | tf_op jit(solution)/shard_map/pallas_call | solution.py:427
Async XLA Ops:
  0.6 4.2 %collective-permute-start = (s32[2,4]{1,0:T(2,128)}, s32[2,4]{1,0:T(2,128)S(1)}, u32[]{:S(2)}, u32[]{:S(2)}) collective-permute-start(s32[2,4]{1,0:T(2,128)} %bitcast.1), channel_id=1, source_target_pairs={{0,8},{8,16},{16,24},{24,32},{32,40},{40,48},{48,56},{56,64},{64,7... | collective-permute-start | bytes 104 | tf_op jit(solution)/shard_map/ppermute | solution.py:446
  4.8 0.5 copy-start

commit v4 on v3

--- a/solution.py
+++ b/solution.py
@@ -12,6 +12,7 @@
 f32, bf16 = jnp.float32, jnp.bfloat16
 phase_scale = 32.0
 TILE, CUTS = "tile", "cuts"
+TURNS = 4
 RIGHT_A, RIGHT_A_CONJ, RIGHT_F, RIGHT_F_CONJ = range(4)
 
 
@@ -38,26 +39,27 @@
     return jnp.dot(a, b, preferred_element_type=f32)
 
 
-def right_times(re, im, table):
+def right_times(re, im, table, turn):
     n = re.shape[1]
     high, low = split(jnp.concatenate([re, im], 1))
-    parts = jnp.concatenate([table[: 2 * n], table[...]], 0)
-    out = dot(jnp.concatenate([low, high, high, high], 1), parts)
+    main = table[: 2 * n]
+    rest = table[pl.ds(pl.multiple_of((turn + 1) * 2 * n, 2 * n), 2 * n), :]
+    out = dot(jnp.concatenate([low, high, high], 1), jnp.concatenate([main, main, rest], 0))
     return out[:, :n], out[:, n:]
 
 
-def left_times(re, im, table):
+def left_times(re, im, table, turn):
     n = re.shape[0]
     high, low = split(jnp.concatenate([re, im], 0))
     main = dot(table[:, : 2 * n], jnp.concatenate([high, low], 1))
-    rest = dot(table[:, 2 * n :], jnp.concatenate([high, high], 0))
+    rest = dot(table[:, pl.ds(pl.multiple_of((turn + 1) * 2 * n, 2 * n), 2 * n)], high)
     out = main[:, :n] + main[:, n:] + rest
     return out[:n], out[n:]
 
 
-def both_sides(re, im, rights, lefts, which):
-    re, im = right_times(re, im, rights.at[which])
-    return left_times(re, im, lefts.at[which])
+def both_sides(re, im, rights, lefts, which, turn):
+    re, im = right_times(re, im, rights.at[which], turn)
+    return left_times(re, im, lefts.at[which], turn)
 
 
 def fused_kernel(
@@ -201,15 +203,9 @@
         own_counts.start()
 
 
-    def take_own(j, carry):
+    def send_windows(j, carry):
         k = turn(j, True)
         window(k, merged, k < half)
-        return carry
-
-    lax.fori_loop(0, count, take_own, 0)
-
-    def send_windows(j, carry):
-        k = turn(j, True)
         rim_copy(k).wait_recv()
         for s in range(slices):
             for i in range(2):
@@ -227,6 +223,7 @@
 
         return carry
 
+    lax.fori_loop(0, count, send_windows, 0)
     for copy in table_loads:
         copy.wait()
 
@@ -235,13 +232,15 @@
         for i in range(blocks.shape[0]):
             which, other = (i // 2) * 2 + i % 2, (i // 2) * 2 + 1 - i % 2
             high = blocks[i].astype(bf16)
-            low, rest = split(blocks[i] - high.astype(f32))
-            for j, part in enumerate((high, low, rest)):
+            rest = blocks[i] - high.astype(f32)
+            parts, taken = [high], jnp.zeros_like(rest)
+            for j in range(TURNS):
+                parts.append((rest * (j + 1.0) - taken).astype(bf16))
+                taken = taken + parts[-1].astype(f32)
+            for j, part in enumerate(parts):
                 at = slice(j * 2 * n, (j + 1) * 2 * n)
                 rights[which, at, :] = part
                 lefts[other, :, at] = part
-
-    lax.fori_loop(0, count, send_windows, 0)
 
     def back_copy(s):
         inner = lax.rem(s, slices)
@@ -262,6 +261,12 @@
         a, b = psi[s, 0], psi[s, 1]
         contrib[s, 0] = a * re + b * im
         contrib[s, 1] = a * im - b * re
+
+        @pl.when(lax.rem(s, slices) == slices - 1)
+        def _():
+            send_terms(s)
+
+    def send_terms(s):
         z = lax.div(s, slices)
 
         @pl.when(z != me)
@@ -300,7 +305,7 @@
 
             a, b = psi[s, 0], psi[s, 1]
             p, q = patch_at(s)
-            re, im = both_sides(p * a - q * b, p * b + q * a, rights, lefts, RIGHT_A)
+            re, im = both_sides(p * a - q * b, p * b + q * a, rights, lefts, RIGHT_A, lax.rem(s, TURNS))
             psi[s + 1, 0] = re
             psi[s + 1, 1] = im
             return carry
@@ -308,7 +313,7 @@
         lax.fori_loop(0, total - 1, forward, 0)
         a, b = psi[total - 1, 0], psi[total - 1, 1]
         p, q = patch_at(total - 1)
-        re, im = both_sides(p * a - q * b, p * b + q * a, rights, lefts, RIGHT_F)
+        re, im = both_sides(p * a - q * b, p * b + q * a, rights, lefts, RIGHT_F, 0)
 
         @pl.when(mine < half)
         def _():
@@ -319,18 +324,25 @@
             next_counts.wait_recv()
 
         weight = 4.0 * (re * re + im * im - counts[...].astype(f32))
-        re, im = both_sides(weight * re, weight * im, rights, lefts, RIGHT_F_CONJ)
+        re, im = both_sides(weight * re, weight * im, rights, lefts, RIGHT_F_CONJ, 0)
         put(total - 1, re, im)
 
         def backward(i, carry):
             re, im = carry
             s = total - 1 - i
             p, q = patch_at(s)
-            re, im = both_sides(p * re + q * im, p * im - q * re, rights, lefts, RIGHT_A_CONJ)
+            re, im = both_sides(p * re + q * im, p * im - q * re, rights, lefts, RIGHT_A_CONJ, lax.rem(i, TURNS))
             put(s - 1, re, im)
             return re, im
 
         lax.fori_loop(0, total - 1, backward, (re, im))
+
+        def send_rest(step, carry):
+            inner = slices - 2 - lax.div(step, cuts)
+            send_terms(lax.rem(me + cuts // 2 + step, cuts) * slices + inner)
+            return carry
+
+        lax.fori_loop(0, cuts * (slices - 1), send_rest, 0)
 
     def term_copy(k, s):
         return pltpu.make_async_remote_copy(
@@ -343,8 +355,8 @@
         )
 
     def pass_on(step, carry):
-        s = slices - 1 - lax.rem(lax.div(step, half), slices)
-        k = turn(lax.div(step, half * slices) * half + lax.rem(step, half), False)
+        s = slices - 1 - lax.div(step, count)
+        k = turn(lax.rem(step, count), False)
 
         @pl.when(owner(k) != me)
         def _():
@@ -394,45 +406,60 @@
         lax.fori_loop(0, total, finish_back, 0)
 
 
-def add_kernel(places, places_before, own, other, real, imag):
-    n = own.shape[-1]
-    count = own.shape[0]
+def add_kernel(places, places_before, own_hbm, other_hbm, real_hbm, imag_hbm, own, other, strip, load_sem, store_sem):
+    count, slices, _, n, _ = own.shape
+    last = strip.shape[3] // n - 1
+    loads = []
+    for s in range(slices):
+        for i, (source, target) in enumerate(((own_hbm, own), (other_hbm, other))):
+            copy = pltpu.make_async_copy(source.at[:, s], target.at[:, s], load_sem.at[s, i])
+            copy.start()
+            loads.append(copy)
+    strip[...] = jnp.zeros_like(strip)
     rows = lax.broadcasted_iota(jnp.int32, (n, n), 0)
     cols = lax.broadcasted_iota(jnp.int32, (n, n), 1)
-    last = real.shape[2] // n - 1
-    real[...] = jnp.zeros_like(real)
-    imag[...] = jnp.zeros_like(imag)
-    for source, first_own in ((own, True), (other, False)):
-        for k in range(count):
-            is_own = (k < count // 2) == first_own
-            where = places if is_own else places_before
-            row = lax.rem(where[0, k], n)
-            column = where[1, k]
-            block = lax.div(column, n)
-            keep = (rows >= row) if is_own else (rows < row)
-            here = pl.ds(pl.multiple_of(block * n, n), n)
-            beside = pl.ds(pl.multiple_of(jnp.minimum(block + 1, last) * n, n), n)
-            first = cols >= column - block * n
-            for i, target in enumerate((real, imag)):
-                value = jnp.where(keep, source[k, 0, i], 0.0)
-                target[0, :, here] += jnp.where(first, value, 0.0)
-                target[0, :, beside] += jnp.where(first, 0.0, value)
+    stores = []
+    for s in range(slices):
+        loads[2 * s].wait()
+        loads[2 * s + 1].wait()
+        for i, target in enumerate((real_hbm, imag_hbm)):
+            for source, first_own in ((own, True), (other, False)):
+                for k in range(count):
+                    is_own = (k < count // 2) == first_own
+                    where = places if is_own else places_before
+                    row = lax.rem(where[0, k], n)
+                    column = where[1, k]
+                    block = lax.div(column, n)
+                    keep = (rows >= row) if is_own else (rows < row)
+                    here = pl.ds(pl.multiple_of(block * n, n), n)
+                    beside = pl.ds(pl.multiple_of(jnp.minimum(block + 1, last) * n, n), n)
+                    first = cols >= column - block * n
+                    value = jnp.where(keep, source[k, s, i], 0.0)
+                    strip[s, i, :, here] += jnp.where(first, value, 0.0)
+                    strip[s, i, :, beside] += jnp.where(first, 0.0, value)
+            copy = pltpu.make_async_copy(strip.at[s, i], target.at[s], store_sem.at[s, i])
+            copy.start()
+            stores.append(copy)
+    for copy in stores:
+        copy.wait()
 
 
 def add(places, places_before, own, other, shape):
     slices, rows, cols = shape
-    count, _, _, n, _ = own.shape
-    window = pl.BlockSpec((count, 1, 2, n, n), lambda s, *_: (0, s, 0, 0, 0))
-    strip = pl.BlockSpec((1, rows, cols), lambda s, *_: (s, 0, 0))
+    smem = pl.BlockSpec(memory_space=pltpu.SMEM)
+    hbm = pl.BlockSpec(memory_space=pltpu.HBM)
     return pl.pallas_call(
         add_kernel,
         out_shape=(jax.ShapeDtypeStruct(shape, f32),) * 2,
-        grid_spec=pltpu.PrefetchScalarGridSpec(
-            num_scalar_prefetch=2,
-            grid=(slices,),
-            in_specs=[window, window],
-            out_specs=(strip, strip),
-        ),
+        in_specs=[smem, smem, hbm, hbm],
+        out_specs=(hbm, hbm),
+        scratch_shapes=[
+            pltpu.VMEM(own.shape, f32),
+            pltpu.VMEM(other.shape, f32),
+            pltpu.VMEM((slices, 2, rows, cols), f32),
+            pltpu.SemaphoreType.DMA((slices, 2)),
+            pltpu.SemaphoreType.DMA((slices, 2)),
+        ],
         compiler_params=pltpu.CompilerParams(vmem_limit_bytes=62 << 20),
     )(places, places_before, own, other)
 
@@ -461,8 +488,8 @@
             pltpu.VMEM(probe.shape, f32),
             pltpu.VMEM((n, n), jnp.int32),
             pltpu.VMEM(blocks.shape, f32),
-            pltpu.VMEM((4, 6 * n, 2 * n), bf16),
-            pltpu.VMEM((4, 2 * n, 6 * n), bf16),
+            pltpu.VMEM((4, (TURNS + 1) * 2 * n, 2 * n), bf16),
+            pltpu.VMEM((4, 2 * n, (TURNS + 1) * 2 * n), bf16),
             pltpu.VMEM(windows, f32),
             pltpu.VMEM(windows, f32),
             pltpu.VMEM(windows, f32),

time: 88.9 us -> 85.4 us (0.961)
  Pallas kernels: 82.8 us -> 79.6 us
    pallas_call x1, Pallas kernels: 78.3 us -> 75.4 us  [shards(): pl.pallas_call(fused_kernel, out_shape=(jax.ShapeDtypeStruct(windows, f32...]
where the time goes in v4:
time: 85.4 us; the launch traced here: 84.9 us
  Pallas kernels  79.6 us (93%)
  starting transfers between devices  2.76 us (3%)
  waiting for transfers between devices  1.4 us (2%)
    pallas_call x1, Pallas kernels, shards(): pl.pallas_call(fused_kernel, out_shape=(jax.ShapeDtypeStruct(windows, f32...  75.4 us
    pallas_call x1, Pallas kernels, add(): pl.pallas_call(add_kernel, out_shape=(jax.ShapeDtypeStruct(shape, f32),)...  4.19 us
    ppermute x1, starting transfers between devices, shards(): lax.ppermute(positions, TILE, [(t, (t + 1) % tiles) for t in range(tiles)])  2.76 us
  transfers between devices with their start and end apart: 1, of which 1 were waited for; matrix products, arithmetic and copies ran while one was open for 0% of the time, Pallas kernels for 0%

profile of v4, /device:TPU:1, one launch (start us, length us, event | category | flops | bytes accessed | tf_op | source)
XLA Modules:
  0.0 84.9 jit_solution(10985530840840121714)
XLA Ops:
  0.6 2.8 %collective-permute-start = (s32[2,4]{1,0:T(2,128)}, s32[2,4]{1,0:T(2,128)S(1)}, u32[]{:S(2)}, u32[]{:S(2)}) collective-permute-start(s32[2,4]{1,0:T(2,128)} %bitcast.1), channel_id=1, source_target_pairs={{0,8},{8,16},{16,24},{24,32},{32,40},{40,48},{48,56},{56,64},{64,7... | collective-permute-start | bytes 104 | tf_op jit(solution)/shard_map/ppermute | solution.py:473
  3.4 1.4 %collective-permute-done.places_before = s32[2,4]{1,0:T(2,128)S(1)} collective-permute-done((s32[2,4]{1,0:T(2,128)}, s32[2,4]{1,0:T(2,128)S(1)}, u32[]{:S(2)}, u32[]{:S(2)}) %collective-permute-start) | collective-permute-done | bytes 64 | tf_op jit(solution)/shard_map/ppermute | solution.py:473
  4.8 0.0 copy-start
  4.8 0.5 copy-done
  5.3 75.4 %shard_map.77 = (f32[4,2,2,128,128]{4,3,2,1,0:T(8,128)}, f32[4,2,2,128,128]{4,3,2,1,0:T(8,128)}) custom-call(s32[2,4]{1,0:T(2,128)} %bitcast.2, s32[2,4]{1,0:T(2,128)} %copy-done, f32[2,128,128]{2,1,0:T(8,128)} %probe_hbm.1, s32[4,128,128]{2,1,0:T(8,128)} %counts_hbm.1, f32[2,128,2048]{2,1,0:T(8,128)} %real_hbm.1, f32[2,128,2048]{2,1,0:T(8,128)} %imag_hbm.1, ...), custom_call_target="tpu_custom_call" | custom-call | tf_op jit(solution)/shard_map/pallas_call | solution.py:480
  80.7 4.2 %shard_map.78 = (f32[2,128,2048]{2,1,0:T(8,128)}, f32[2,128,2048]{2,1,0:T(8,128)}) custom-call(s32[2,4]{1,0:T(2,128)} %bitcast.3, s32[2,4]{1,0:T(2,128)} %copy-done, f32[4,2,2,128,128]{4,3,2,1,0:T(8,128)} %get-tuple-element.4.own_hbm, f32[4,2,2,128,128]{4,3,2,1,0:T(8,128)} %get-tuple-element.5.other_hbm), custom_call_target="tpu_custom_call" | custom-call | tf_op jit(solution)/shard_map/pallas_call | solution.py:451
Async XLA Ops:
  0.6 4.2 %collective-permute-start = (s32[2,4]{1,0:T(2,128)}, s32[2,4]{1,0:T(2,128)S(1)}, u32[]{:S(2)}, u32[]{:S(2)}) collective-permute-start(s32[2,4]{1,0:T(2,128)} %bitcast.1), channel_id=1, source_target_pairs={{0,8},{8,16},{16,24},{24,32},{32,40},{40,48},{48,56},{56,64},{64,7... | collective-permute-start | bytes 104 | tf_op jit(solution)/shard_map/ppermute | solution.py:473
  4.8 0.5 copy-start

commit v5 on v4

--- a/solution.py
+++ b/solution.py
@@ -172,14 +172,14 @@
     def owner(k):
         return lax.rem(k * spread + phase, cuts)
 
-    def gather_copy(k):
+    def gather_copy(k, s):
         return pltpu.make_async_remote_copy(
-            merged.at[k], patches.at[me], gather_send.at[k], gather_recv.at[me], **device(tile, owner(k))
-        )
-
-    def arrival(z):
+            merged.at[k, s], patches.at[me, s], gather_send.at[k, s], gather_recv.at[me, s], **device(tile, owner(k))
+        )
+
+    def arrival(z, s):
         return pltpu.make_async_remote_copy(
-            merged.at[0], patches.at[z], gather_send.at[0], gather_recv.at[z], **device(tile, z)
+            merged.at[0, s], patches.at[z, s], gather_send.at[0, s], gather_recv.at[z, s], **device(tile, z)
         )
 
     for copy in loads:
@@ -213,7 +213,8 @@
 
         @pl.when(owner(k) != me)
         def _():
-            gather_copy(k).start()
+            for s in range(slices):
+                gather_copy(k, s).start()
 
         @pl.when(owner(k) == me)
         def _():
@@ -299,9 +300,9 @@
         def forward(s, carry):
             z = lax.div(s, slices)
 
-            @pl.when((lax.rem(s, slices) == 0) & (z != me))
+            @pl.when(z != me)
             def _():
-                arrival(z).wait_recv()
+                arrival(z, lax.rem(s, slices)).wait_recv()
 
             a, b = psi[s, 0], psi[s, 1]
             p, q = patch_at(s)
@@ -311,6 +312,11 @@
             return carry
 
         lax.fori_loop(0, total - 1, forward, 0)
+
+        @pl.when(me != cuts - 1)
+        def _():
+            arrival(cuts - 1, slices - 1).wait_recv()
+
         a, b = psi[total - 1, 0], psi[total - 1, 1]
         p, q = patch_at(total - 1)
         re, im = both_sides(p * a - q * b, p * b + q * a, rights, lefts, RIGHT_F, 0)
@@ -383,7 +389,8 @@
 
         @pl.when(owner(k) != me)
         def _():
-            gather_copy(k).wait_send()
+            for s in range(slices):
+                gather_copy(k, s).wait_send()
 
         return carry
 
@@ -502,8 +509,8 @@
             dma((1,)),
             dma((count,)),
             dma((count,)),
-            dma((count,)),
-            dma((cuts,)),
+            dma((count, slices)),
+            dma((cuts, slices)),
             dma((total,)),
             dma((count, slices)),
             dma((count, slices)),

time: 85.4 us -> 85 us (level)
  no operation moved by 1% of the time
where the time goes in v5:
time: 85 us; the launch traced here: 84.5 us
  Pallas kernels  79.2 us (93%)
  starting transfers between devices  2.76 us (3%)
  waiting for transfers between devices  1.4 us (2%)
    pallas_call x1, Pallas kernels, shards(): pl.pallas_call(fused_kernel, out_shape=(jax.ShapeDtypeStruct(windows, f32...  75 us
    pallas_call x1, Pallas kernels, add(): pl.pallas_call(add_kernel, out_shape=(jax.ShapeDtypeStruct(shape, f32),)...  4.19 us
    ppermute x1, starting transfers between devices, shards(): lax.ppermute(positions, TILE, [(t, (t + 1) % tiles) for t in range(tiles)])  2.76 us
  transfers between devices with their start and end apart: 1, of which 1 were waited for; matrix products, arithmetic and copies ran while one was open for 0% of the time, Pallas kernels for 0%

profile of v5, /device:TPU:1, one launch (start us, length us, event | category | flops | bytes accessed | tf_op | source)
XLA Modules:
  0.0 84.5 jit_solution(14074154708029627163)
XLA Ops:
  0.6 2.8 %collective-permute-start = (s32[2,4]{1,0:T(2,128)}, s32[2,4]{1,0:T(2,128)S(1)}, u32[]{:S(2)}, u32[]{:S(2)}) collective-permute-start(s32[2,4]{1,0:T(2,128)} %bitcast.1), channel_id=1, source_target_pairs={{0,8},{8,16},{16,24},{24,32},{32,40},{40,48},{48,56},{56,64},{64,7... | collective-permute-start | bytes 104 | tf_op jit(solution)/shard_map/ppermute | solution.py:480
  3.4 1.4 %collective-permute-done.places_before = s32[2,4]{1,0:T(2,128)S(1)} collective-permute-done((s32[2,4]{1,0:T(2,128)}, s32[2,4]{1,0:T(2,128)S(1)}, u32[]{:S(2)}, u32[]{:S(2)}) %collective-permute-start) | collective-permute-done | bytes 64 | tf_op jit(solution)/shard_map/ppermute | solution.py:480
  4.8 0.0 copy-start
  4.8 0.5 copy-done
  5.3 75.0 %shard_map.77 = (f32[4,2,2,128,128]{4,3,2,1,0:T(8,128)}, f32[4,2,2,128,128]{4,3,2,1,0:T(8,128)}) custom-call(s32[2,4]{1,0:T(2,128)} %bitcast.2, s32[2,4]{1,0:T(2,128)} %copy-done, f32[2,128,128]{2,1,0:T(8,128)} %probe_hbm.1, s32[4,128,128]{2,1,0:T(8,128)} %counts_hbm.1, f32[2,128,2048]{2,1,0:T(8,128)} %real_hbm.1, f32[2,128,2048]{2,1,0:T(8,128)} %imag_hbm.1, ...), custom_call_target="tpu_custom_call" | custom-call | tf_op jit(solution)/shard_map/pallas_call | solution.py:487
  80.3 4.2 %shard_map.78 = (f32[2,128,2048]{2,1,0:T(8,128)}, f32[2,128,2048]{2,1,0:T(8,128)}) custom-call(s32[2,4]{1,0:T(2,128)} %bitcast.3, s32[2,4]{1,0:T(2,128)} %copy-done, f32[4,2,2,128,128]{4,3,2,1,0:T(8,128)} %get-tuple-element.4.own_hbm, f32[4,2,2,128,128]{4,3,2,1,0:T(8,128)} %get-tuple-element.5.other_hbm), custom_call_target="tpu_custom_call" | custom-call | tf_op jit(solution)/shard_map/pallas_call | solution.py:458
Async XLA Ops:
  0.6 4.2 %collective-permute-start = (s32[2,4]{1,0:T(2,128)}, s32[2,4]{1,0:T(2,128)S(1)}, u32[]{:S(2)}, u32[]{:S(2)}) collective-permute-start(s32[2,4]{1,0:T(2,128)} %bitcast.1), channel_id=1, source_target_pairs={{0,8},{8,16},{16,24},{24,32},{32,40},{40,48},{48,56},{56,64},{64,7... | collective-permute-start | bytes 104 | tf_op jit(solution)/shard_map/ppermute | solution.py:480
  4.8 0.5 copy-start
